TPU v7x, 256 devices: a whole 4x4x8 slice. The times are simulated.
256 devices in a mesh: hier: 4 (over x), row: 64 (over z, y, core).
Axes of the slice: x: 4, y: 4, z: 8, core: 2. Of those that a mesh axis runs over, the one named last changes fastest.
Arguments:
- rho: float32 [64, 2, 1024, 1024], P('hier', None, 'row'), may hold values from -6 to 6
- incr: float32 [64, 2, 1024, 1024], P('hier', None, 'row'), may hold values from -6 to 6
- accum: float32 [64, 2, 1024, 1024], P('hier', None, 'row'), may hold values from -6 to 6
- ham: float32 [1024, 1024], P('row'), as said below
- modes: float32 [8, 1024], replicated, may hold values from -4 to 4
- coeff: float32 [2, 8], replicated, may hold values from 0.2 to 1
- damping: float32 [64], P('hier'), may hold values from 0.1 to 3
- links: int32 [64, 4], replicated, may hold values from 0 to 63, as said below
- bath: int32 [64, 4], replicated, may hold values from 0 to 7
- kinds: int32 [64, 4], replicated, may hold values from 0 to 2
Outputs:
- deriv: float32 [64, 2, 1024, 1024], P('hier', None, 'row')
- accum_new: float32 [64, 2, 1024, 1024], P('hier', None, 'row')
Inputs may be any that keep to these rules, and one draw needn't show every extreme that they name: ham is exactly symmetric. `links`: an unused slot names its own matrix. For every two different hierarchy groups g and h (matrices g * 16 to (g + 1) * 16 - 1 form group g), the used slots of g's matrices name exactly 4 distinct matrices of group h.
All inputs are finite; a program needn't handle non-finite values.
Results may differ from a plain program's by a relative error of at most 0.0003.
Values sent between devices are 32-bit elements; how exact they have to be, the bound alone decides.
A program may use at most 128 MiB of HBM per device.

v0:
```python
import jax
import jax.numpy as jnp
from jax import lax
from jax.sharding import PartitionSpec as P

half_step = 0.1
third_step = 0.2 / 3.0


def local(rho, incr, accum, ham, modes, coeff, damping, links, bath, kinds):
    group_aux = rho.shape[0]
    panel_rows = rho.shape[2]
    order_size = rho.shape[3]
    owners = lax.axis_size("row")
    group_index = lax.axis_index("hier")
    aux_base = group_index * group_aux
    row_base = lax.axis_index("row") * panel_rows
    section_arg = rho + half_step * incr
    full_ham = lax.all_gather(ham, "row", axis=0, tiled=True)
    right_prod = jnp.einsum("apri,is->aprs", section_arg, full_ham, precision=lax.Precision.HIGHEST)
    tile_rows = section_arg.reshape(group_aux, 2, panel_rows, owners, panel_rows)
    tile_rows = tile_rows.transpose(0, 1, 3, 4, 2).reshape(
        group_aux, 2, owners, panel_rows * panel_rows
    )
    ham_blocks = full_ham.reshape(owners, panel_rows, order_size)
    arrived = lax.all_to_all(tile_rows, "row", split_axis=2, concat_axis=2, tiled=True)
    items = arrived.shape[0]
    blocks = arrived.reshape(items, 2, owners, panel_rows, panel_rows)
    product = jnp.einsum("apdcr,drs->apcs", blocks, ham_blocks, precision=lax.Precision.HIGHEST)
    outgoing = product.reshape(items, 2, panel_rows, owners, panel_rows)
    outgoing = outgoing.transpose(0, 1, 3, 4, 2).reshape(items, 2, owners, panel_rows * panel_rows)
    returned = lax.all_to_all(outgoing, "row", split_axis=2, concat_axis=2, tiled=True)
    returned = returned.reshape(items, 2, owners, panel_rows, panel_rows)
    left_prod = returned.transpose(0, 1, 3, 2, 4).reshape(items, 2, panel_rows, order_size)
    commutator = left_prod - right_prod
    deriv = (
        jnp.stack([commutator[:, 1], -commutator[:, 0]], axis=1)
        - damping[:, None, None, None] * section_arg
    )
    own_links = lax.dynamic_slice_in_dim(links, aux_base, group_aux, 0)
    own_bath = lax.dynamic_slice_in_dim(bath, aux_base, group_aux, 0)
    own_kinds = lax.dynamic_slice_in_dim(kinds, aux_base, group_aux, 0)
    panel_pool = lax.all_gather(section_arg, "hier", axis=0, tiled=True)
    bath_range = jnp.arange(modes.shape[0], dtype=jnp.int32)
    for slot in range(links.shape[1]):
        neighbour = jnp.take(panel_pool, own_links[:, slot], axis=0)
        onehot = (own_bath[:, slot][:, None] == bath_range[None, :]).astype(jnp.float32)
        col_weights = jnp.dot(onehot, modes, precision=lax.Precision.HIGHEST)
        row_weights = lax.dynamic_slice_in_dim(col_weights, row_base, panel_rows, 1)
        coef_real = jnp.dot(onehot, coeff[0], precision=lax.Precision.HIGHEST)
        coef_imag = jnp.dot(onehot, coeff[1], precision=lax.Precision.HIGHEST)
        kind_now = own_kinds[:, slot]
        raising = (kind_now == 1).astype(jnp.float32)
        lowering = (kind_now == 2).astype(jnp.float32)
        direct = (raising + lowering * coef_real)[:, None, None]
        mixing = (lowering * coef_imag)[:, None, None]
        gap_field = row_weights[:, :, None] - col_weights[:, None, :]
        sum_field = row_weights[:, :, None] + col_weights[:, None, :]
        real_term = direct * gap_field * neighbour[:, 1] + mixing * sum_field * neighbour[:, 0]
        imag_term = -(direct * gap_field * neighbour[:, 0]) + mixing * sum_field * neighbour[:, 1]
        deriv = deriv + jnp.stack([real_term, imag_term], axis=1)
    return (deriv, accum + third_step * deriv)


def solution(mesh):
    in_specs = (
        P("hier", None, "row", None),
        P("hier", None, "row", None),
        P("hier", None, "row", None),
        P("row", None),
        P(),
        P(),
        P("hier"),
        P(),
        P(),
        P(),
    )
    out_specs = (P("hier", None, "row", None), P("hier", None, "row", None))
    return jax.shard_map(local, mesh=mesh, in_specs=in_specs, out_specs=out_specs, check_vma=False)
```

profile of v0, /device:TPU:1, one launch (start us, length us, event | category | flops | bytes accessed | tf_op | source)
XLA Modules:
  0.0 314.9 jit_solution(11980416151194248368)
XLA Ops:
  8.0 4.2 %multiply_add_fusion.1 = f32[16,2,16,1024]{3,2,1,0:T(8,128)} fusion(f32[16,2,16,1024]{3,2,1,0:T(8,128)} %param.12, f32[16,2,16,1024]{3,2,1,0:T(8,128)} %param.13), kind=kLoop, calls=%fused_computation.15 | loop fusion | flops 1048576 | bytes 6291456 | tf_op jit(solution)/shard_map/add | solution.py:18
  13.7 9.0 %reshape.121 = f32[16,2,16,64,16]{4,3,2,1,0:T(8,128)} reshape(f32[16,2,16,1024]{3,2,1,0:T(8,128)S(1)} %copy-done.2) | data formatting | bytes 4194304 | tf_op jit(solution)/shard_map/reshape | solution.py:21
  22.7 11.4 %copy.22 = f32[16,2,64,16,16]{2,4,3,1,0:T(8,128)} copy(f32[16,2,64,16,16]{3,2,4,1,0:T(8,128)} %bitcast.144) | data formatting | bytes 4194304 | tf_op jit(solution)/shard_map/transpose | solution.py:22
  34.2 4.2 %copy.23 = f32[16,2,64,256]{3,0,1,2:T(8,128)} copy(f32[16,2,64,256]{2,3,1,0:T(8,128)} %bitcast.146) | data formatting | bytes 4194304 | tf_op jit(solution)/shard_map/reshape | solution.py:22
  38.3 13.6 %all-to-all-start = ((f32[16,2,64,256]{3,0,1,2:T(8,128)}), f32[16,2,64,256]{3,0,1,2:T(8,128)}, u32[]{:S(2)}, u32[]{:S(2)}) async-start(f32[16,2,64,256]{3,0,1,2:T(8,128)} %copy.23), calls=%async_computation | async-start | bytes 4194304 | tf_op jit(solution)/shard_map/all_to_all | solution.py:26
  52.0 59.3 %all-to-all-done = f32[16,2,64,256]{3,0,1,2:T(8,128)} async-done(((f32[16,2,64,256]{3,0,1,2:T(8,128)}), f32[16,2,64,256]{3,0,1,2:T(8,128)}, u32[]{:S(2)}, u32[]{:S(2)}) %all-to-all-start) | async-done | bytes 2097184 | tf_op jit(solution)/shard_map/all_to_all | solution.py:26
  111.4 3.8 %copy.24 = f32[16,2,64,256]{2,3,1,0:T(8,128)} copy(f32[16,2,64,256]{3,0,1,2:T(8,128)} %all-to-all-done) | data formatting | bytes 4194304 | tf_op jit(solution)/shard_map/all_to_all | solution.py:26
  115.2 8.8 %copy.25 = f32[64,16,1024]{0,1,2:T(8,128)} copy(f32[64,16,1024]{2,1,0:T(8,128)} %bitcast.145) | data formatting | bytes 8388608 | tf_op jit(solution)/shard_map/reshape | solution.py:25
  124.0 40.0 %fusion = f32[16,2,16,64,16,1]{3,2,5,4,1,0:T(8,128)} fusion(f32[64,16,64,16,1,1]{2,3,1,0,5,4:T(8,128)} %bitcast.148, f32[16,2,64,16,16,1]{2,4,3,1,0,5:T(8,128)} %bitcast.149), kind=kOutput, calls=%fused_computation.4 | convolution fusion | flops 6442450944 | bytes 8388608 | tf_op jit(solution)/shard_map/apdcr,drs->apcs/dot_general | solution.py:29
  164.1 4.2 %copy.28 = f32[16,2,64,256]{3,0,1,2:T(8,128)} copy(f32[16,2,64,256]{2,3,1,0:T(8,128)} %bitcast.150) | data formatting | bytes 4194304 | tf_op jit(solution)/shard_map/reshape | solution.py:31
  168.2 7.2 %all-to-all-start.1 = ((f32[16,2,64,256]{3,0,1,2:T(8,128)}), f32[16,2,64,256]{3,0,1,2:T(8,128)}, u32[]{:S(2)}, u32[]{:S(2)}) async-start(f32[16,2,64,256]{3,0,1,2:T(8,128)} %copy.28), calls=%async_computation.1 | async-start | bytes 4194304 | tf_op jit(solution)/shard_map/all_to_all | solution.py:32
  178.4 46.6 %all-to-all-done.1 = f32[16,2,64,256]{3,0,1,2:T(8,128)} async-done(((f32[16,2,64,256]{3,0,1,2:T(8,128)}), f32[16,2,64,256]{3,0,1,2:T(8,128)}, u32[]{:S(2)}, u32[]{:S(2)}) %all-to-all-start.1) | async-done | bytes 2097184 | tf_op jit(solution)/shard_map/all_to_all | solution.py:32
  225.0 3.8 %copy.29 = f32[16,2,64,256]{2,3,1,0:T(8,128)} copy(f32[16,2,64,256]{3,0,1,2:T(8,128)} %all-to-all-done.1) | data formatting | bytes 4194304 | tf_op jit(solution)/shard_map/all_to_all | solution.py:32
  228.8 10.5 %copy.30 = f32[16,2,16,64,16]{4,3,2,1,0:T(8,128)} copy(f32[16,2,16,64,16]{3,4,2,1,0:T(8,128)} %bitcast.147) | data formatting | bytes 4194304 | tf_op jit(solution)/shard_map/transpose | solution.py:34
  239.4 15.2 %reshape.127 = f32[16,2,16,1024]{3,2,1,0:T(8,128)} reshape(f32[16,2,16,64,16]{4,3,2,1,0:T(8,128)} %copy.30) | data formatting | bytes 4194304 | tf_op jit(solution)/shard_map/reshape | solution.py:34
  254.6 9.4 %fusion.9 = f32[16,2,16,1024]{3,2,1,0:T(8,128)S(1)} fusion(f32[16,2,16,1024]{3,2,1,0:T(8,128)} %reshape.127, f32[16,2,16,1024]{3,2,1,0:T(8,128)S(1)} %copy-done.2, f32[1024,1024]{1,0:T(8,128)} %all-gather.3.cloned.1.call-done), kind=kOutput, calls=%fused_computation.16 | convolution fusion | flops 6442975232 | bytes 10485760 | tf_op jit(solution)/shard_map/apri,is->aprs/dot_general | solution.py:20
  265.2 5.4 %gather_fusion = f32[16,2,16,1024]{3,2,1,0:T(8,128)} fusion(f32[64,2,16,1024]{3,2,1,0:T(8,128)} %all-gather.5.cloned.1.call-done, s32[1024]{0:T(1024)S(1)} %pad_clamp_fusion.3), kind=kCustom, calls=%fused_computation.clone | custom fusion | bytes 4194368 | tf_op jit(solution)/shard_map/jit(_take)/gather | solution.py:46
  270.6 3.3 %broadcast_select_fusion.3 = f32[16,2,16,1024]{3,2,1,0:T(8,128)} fusion(f32[16,2,16,1024]{3,2,1,0:T(8,128)} %gather_fusion, pred[16]{0:T(512)(128)(4,1)S(1)} %get-tuple-element.11), kind=kLoop, calls=%fused_computation.41 | loop fusion | flops 524288 | bytes 4194320 | tf_op jit(solution)/shard_map/jit(_take)/select_n | solution.py:46
  273.9 5.4 %gather_fusion.1 = f32[16,2,16,1024]{3,2,1,0:T(8,128)} fusion(f32[64,2,16,1024]{3,2,1,0:T(8,128)} %all-gather.5.cloned.1.call-done, s32[1024]{0:T(1024)S(1)} %pad_clamp_fusion.2), kind=kCustom, calls=%fused_computation.1.clone | custom fusion | bytes 4194368 | tf_op jit(solution)/shard_map/jit(_take)/gather | solution.py:46
  279.3 3.3 %broadcast_select_fusion.2 = f32[16,2,16,1024]{3,2,1,0:T(8,128)} fusion(f32[16,2,16,1024]{3,2,1,0:T(8,128)} %gather_fusion.1, pred[16]{0:T(512)(128)(4,1)S(1)} %get-tuple-element.31), kind=kLoop, calls=%fused_computation.40 | loop fusion | flops 524288 | bytes 4194320 | tf_op jit(solution)/shard_map/jit(_take)/select_n | solution.py:46
  282.6 5.4 %gather_fusion.2 = f32[16,2,16,1024]{3,2,1,0:T(8,128)} fusion(f32[64,2,16,1024]{3,2,1,0:T(8,128)} %all-gather.5.cloned.1.call-done, s32[1024]{0:T(1024)S(1)} %pad_clamp_fusion.1), kind=kCustom, calls=%fused_computation.2.clone | custom fusion | bytes 4194368 | tf_op jit(solution)/shard_map/jit(_take)/gather | solution.py:46
  288.0 3.3 %broadcast_select_fusion.1 = f32[16,2,16,1024]{3,2,1,0:T(8,128)} fusion(f32[16,2,16,1024]{3,2,1,0:T(8,128)} %gather_fusion.2, pred[16]{0:T(512)(128)(4,1)S(1)} %get-tuple-element.29), kind=kLoop, calls=%fused_computation.39 | loop fusion | flops 524288 | bytes 4194320 | tf_op jit(solution)/shard_map/jit(_take)/select_n | solution.py:46
  291.3 5.4 %gather_fusion.3 = f32[16,2,16,1024]{3,2,1,0:T(8,128)} fusion(f32[64,2,16,1024]{3,2,1,0:T(8,128)} %all-gather.5.cloned.1.call-done, s32[1024]{0:T(1024)S(1)} %pad_clamp_fusion), kind=kCustom, calls=%fused_computation.3.clone | custom fusion | bytes 4194368 | tf_op jit(solution)/shard_map/jit(_take)/gather | solution.py:46
  304.6 3.4 %multiply_add_fusion = (f32[16,2,16,1024]{3,2,1,0:T(8,128)}, f32[16,2,16,1024]{3,2,1,0:T(8,128)}) fusion(f32[16,2,16,1024]{3,2,1,0:T(8,128)S(1)} %copy-done.7, f32[16,1,16,1024]{3,2,1,0:T(8,128)S(1)} %get-tuple-element.20, f32[16,1,16,1024]{3,2,1,0:T(8,128)S(1)} %get-tuple-element.19, f32[16,1,16,1024]{3,2,1,0:T(8,128)S(1)} %get-tuple-element.18, ...), kind=kLoop, calls=%fused_computation.14 | loop fusion | flops 6815744 | bytes 18874432 | tf_op jit(solution)/shard_map/add | solution.py:62
  (62 shorter events, 14.4 us)
Async XLA Ops:
  7.2 168.5 %copy-start = (f32[8,1024]{1,0:T(8,128)S(1)}, f32[8,1024]{1,0:T(8,128)}, u32[]{:S(2)}) copy-start(f32[8,1024]{1,0:T(8,128)} %param.16) | copy-start | bytes 98308
  7.2 108.0 %all-gather.3.cloned.1.call-start = ((), (), s32[]{:S(2)}) async-start(), calls=%async_computation.2 | async-start | bytes 4259840 | tf_op jit(solution)/shard_map/all_gather | solution.py:19
  7.9 257.3 %all-gather.5.cloned.1.call-start = ((), (), s32[]{:S(2)}) async-start(), calls=%async_computation.3 | async-start | bytes 10485760 | tf_op jit(solution)/shard_map/all_gather | solution.py:43
  12.1 1.6 copy-start.2
  38.3 13.6 %copy-start.8 = (s32[64,4]{0,1:T(4,128)S(1)}, s32[64,4]{0,1:T(4,128)}, u32[]{:S(2)}) copy-start(s32[64,4]{0,1:T(4,128)} %param.19) | copy-start | bytes 3076
  38.3 13.6 %copy-start.9 = (s32[64,4]{0,1:T(4,128)S(1)}, s32[64,4]{0,1:T(4,128)}, u32[]{:S(2)}) copy-start(s32[64,4]{0,1:T(4,128)} %param.20) | copy-start | bytes 3076
  38.3 73.0 %all-to-all-start = ((f32[16,2,64,256]{3,0,1,2:T(8,128)}), f32[16,2,64,256]{3,0,1,2:T(8,128)}, u32[]{:S(2)}, u32[]{:S(2)}) async-start(f32[16,2,64,256]{3,0,1,2:T(8,128)} %copy.23), calls=%async_computation | async-start | bytes 4194304 | tf_op jit(solution)/shard_map/all_to_all | solution.py:26
  168.2 7.2 %copy-start.10 = (s32[64,4]{0,1:T(4,128)S(1)}, s32[64,4]{0,1:T(4,128)}, u32[]{:S(2)}) copy-start(s32[64,4]{0,1:T(4,128)} %param.21) | copy-start | bytes 3076
  168.2 8.6 %copy-start.12 = (f32[2,8]{1,0:T(2,128)S(1)}, f32[2,8]{1,0:T(2,128)}, u32[]{:S(2)}) copy-start(f32[2,8]{1,0:T(2,128)} %param.17) | copy-start | bytes 196
  168.2 56.8 %all-to-all-start.1 = ((f32[16,2,64,256]{3,0,1,2:T(8,128)}), f32[16,2,64,256]{3,0,1,2:T(8,128)}, u32[]{:S(2)}, u32[]{:S(2)}) async-start(f32[16,2,64,256]{3,0,1,2:T(8,128)} %copy.28), calls=%async_computation.1 | async-start | bytes 4194304 | tf_op jit(solution)/shard_map/all_to_all | solution.py:32
  296.6 2.2 copy-start.5
  298.9 1.6 copy-start.4
  300.5 1.6 copy-start.3
  302.6 1.2 copy-start.6
  302.7 1.9 copy-start.7
  302.7 1.9 copy-start.11
  304.6 3.4 %copy-start.1 = (f32[8,1024]{1,0:T(8,128)S(1)}, f32[8,1024]{1,0:T(8,128)}, u32[]{:S(2)}) copy-start(f32[8,1024]{1,0:T(8,128)} %param.16) | copy-start | bytes 98308
Sparse Core Ops, SparseCore 0:
  10.8 95.7 all-gather.2
  109.0 84.3 all-gather.4
where the time goes:
time: 317 us; the launch traced here: 315 us
  waiting for transfers between devices  107 us (34%)
  local copies, waits for them, and re-layouts  98.1 us (31%)
  matrix products  51.8 us (16%)
  other arithmetic  23.1 us (7%)
  starting transfers between devices  20.8 us (7%)
  between operations  14.3 us (5%)
    all_to_all x1, waiting for transfers between devices, local(): lax.all_to_all(tile_rows, 'row', split_axis=2, concat_axis=2, tiled=True)  59.3 us
    all_to_all x1, waiting for transfers between devices, local(): lax.all_to_all(outgoing, 'row', split_axis=2, concat_axis=2, tiled=True)  46.6 us
    dot_general x1, matrix products, local(): jnp.einsum('apdcr,drs->apcs', blocks, ham_blocks, precision=lax.Precision...  40 us
    gather x4, local copies, waits for them, and re-layouts, local(): neighbour = jnp.take(panel_pool, own_links[:, slot], axis=0)  21.5 us
    reshape x1, local copies, waits for them, and re-layouts, local(): returned.transpose(0, 1, 3, 2, 4).reshape(items, 2, panel_rows, order_size)  15.2 us
    all_to_all x1, starting transfers between devices, local(): lax.all_to_all(tile_rows, 'row', split_axis=2, concat_axis=2, tiled=True)  13.6 us
    select_n x4, other arithmetic, local(): neighbour = jnp.take(panel_pool, own_links[:, slot], axis=0)  11.9 us
    transpose x1, local copies, waits for them, and re-layouts, local(): tile_rows.transpose(0, 1, 3, 4, 2)  11.4 us
  transfers between devices with their start and end apart: 4, of which 2 were waited for; matrix products, arithmetic and copies ran while one was open for 41% of the time, Pallas kernels for 0%

commit v1 on v0

v1 whole, which is shorter than its diff:
```python
import jax
import jax.numpy as jnp
from jax import lax
from jax.experimental import pallas as pl
from jax.experimental.pallas import tpu as pltpu
from jax.sharding import PartitionSpec as P

half_step = 0.1
third_step = 0.2 / 3.0

MESH = pl.DeviceIdType.MESH
GROUPS = 4
ZS = 8
YS = 4
YC = 8
OWN = 16
CAP = 4
MATS = 32
ROWS = 16
N = 1024
BATH = 8
SLOTS = 4
CHUNKS = 4
WIDE = N // CHUNKS
HALF = WIDE // 2
QUART = N // GROUPS
TILE = 256


def split(x):
    hi = x.astype(jnp.bfloat16)
    return hi, (x - hi.astype(jnp.float32)).astype(jnp.bfloat16)


def dot(a, b):
    return jnp.dot(a, b, preferred_element_type=jnp.float32)


def sorted_links(links_vec, rows_of, target):
    block = links_vec[pl.ds(pl.multiple_of(rows_of * OWN, OWN), OWN), :]
    low = target * OWN
    found, last = [], low - 1
    for _ in range(CAP):
        inside = (block > last) & (block < low + OWN)
        last = jnp.minimum(jnp.min(jnp.where(inside, block, low + OWN - 1)), low + OWN - 1)
        found.append(last)
    return found


def kernel(
    rho, incr, ham, modes, links_vec, coeff, damping, links, bath, kinds,
    deriv,
    panels, rho_buf, incr_buf, ham_buf, ham_hi, ham_lo, z_in, y_in, right_cat, left, y_back, z_back,
    acc, pool, picked, gap, total,
    load_sem, h1_send, h1_recv, h2_send, h2_recv, h3_send, h3_recv, h4_send, h4_recv,
    zi_send, zi_recv, yi_send, yi_recv, yb_send, yb_recv, zb_send, zb_recv, pick_send, pick_recv, out_sem,
):
    h = lax.axis_index("hier")
    r = lax.axis_index("row")
    z = r // YC
    yc = r % YC
    y = yc // 2
    c = yc % 2

    def remote(src, dst, send, recv, group, row):
        return pltpu.make_async_remote_copy(
            src_ref=src, dst_ref=dst, send_sem=send, recv_sem=recv,
            device_id=(group, row), device_id_type=MESH,
        )

    def wait_bytes(ref, sem):
        pltpu.make_async_copy(ref, ref, sem).wait()

    def other_z(k):
        there = (z + k) % ZS
        return there, there * YC + yc

    def other_yc(k):
        there = (yc + k) % YC
        return there, z * YC + there

    def each(first, last, body):
        def step(k, carry):
            body(k)
            return carry

        lax.fori_loop(first, last, step, 0)

    load_rho = pltpu.make_async_copy(rho, rho_buf, load_sem.at[0])
    load_incr = pltpu.make_async_copy(incr, incr_buf, load_sem.at[1])
    load_rho.start()
    load_incr.start()
    barrier = pltpu.get_barrier_semaphore()

    def greet(group, row):
        pl.semaphore_signal(barrier, inc=1, device_id=(group, row), device_id_type=MESH)

    each(1, ZS, lambda k: greet(h, other_z(k)[1]))
    each(1, YC, lambda k: greet(h, other_yc(k)[1]))
    each(1, GROUPS, lambda k: greet((h + k) % GROUPS, r))

    load_rho.wait()
    load_incr.wait()

    def make_panel(m):
        value = rho_buf[m] + half_step * incr_buf[m]
        panels[m] = value
        pool[m] = value

    each(0, MATS, make_panel)
    pl.semaphore_wait(barrier, ZS - 1 + YC - 1 + GROUPS - 1)

    ham_own = ham.at[:, pl.ds(pl.multiple_of(h * QUART, QUART), QUART)]
    h1_local = pltpu.make_async_copy(ham_own, ham_buf.at[h, c, z, y], h1_recv)
    h1_local.start()
    each(1, ZS, lambda k: remote(ham_own, ham_buf.at[h, c, z, y], h1_send, h1_recv, h, other_z(k)[1]).start())

    for j in range(CHUNKS):
        cols = pl.ds(j * WIDE, WIDE)

        def send_z(k, j=j, cols=cols):
            there, row = other_z(k)
            remote(
                panels.at[pl.ds(there * YS, YS), :, cols], z_in.at[j, z], zi_send.at[j], zi_recv.at[j], h, row
            ).start()

        pltpu.make_async_copy(panels.at[pl.ds(z * YS, YS), :, cols], z_in.at[j, z], zi_recv.at[j]).start()
        each(1, ZS, send_z)

    wait_bytes(ham_buf.at[h, c, :, y], h1_recv)
    own_y = ham_buf.at[h, c, :, y]
    each(1, YS, lambda k: remote(own_y, own_y, h2_send, h2_recv, h, z * YC + (y + k) % YS * 2 + c).start())

    for d in range(1, GROUPS):
        chosen = sorted_links(links_vec, (h + d) % GROUPS, h)
        for i in range(CAP):
            place = (chosen[i] - h * OWN) * 2
            picked[d - 1, 2 * i] = panels[place]
            picked[d - 1, 2 * i + 1] = panels[place + 1]

    wait_bytes(ham_buf.at[h, c, :, pl.ds(0, YS - 1)], h2_recv)
    for d in (1, 3, 2):
        remote(
            ham_buf.at[h, c], ham_buf.at[h, c], h3_send.at[d - 1], h3_recv.at[d - 1], (h + d) % GROUPS, r
        ).start()

    def to_core(d):
        quarter = ham_buf.at[(h + GROUPS - d) % GROUPS, c]
        return remote(quarter, quarter, h4_send.at[d], h4_recv.at[d], h, r - c + 1 - c)

    to_core(0).start()
    for d in (1, 3, 2):
        remote(
            picked.at[d - 1], pool.at[pl.ds(MATS + (d - 1) * 2 * CAP, 2 * CAP)],
            pick_send.at[d - 1], pick_recv.at[d - 1], (h + d) % GROUPS, r,
        ).start()

    def forward_in(j):
        wait_bytes(z_in.at[j], zi_recv.at[j])

        def send_y(k):
            there, row = other_yc(k)
            remote(
                z_in.at[j, :, there // 2, :, pl.ds(pl.multiple_of(there % 2 * HALF, HALF), HALF)],
                y_in.at[j, :, yc], yi_send.at[j], yi_recv.at[j], h, row,
            ).start()

        pltpu.make_async_copy(
            z_in.at[j, :, y, :, pl.ds(pl.multiple_of(c * HALF, HALF), HALF)], y_in.at[j, :, yc], yi_recv.at[j]
        ).start()
        each(1, YC, send_y)

    def take_ham(d):
        q = (h + GROUPS - d) % GROUPS
        wait_bytes(ham_buf.at[q, 1 - c], h4_recv.at[d])
        cols = pl.ds(pl.multiple_of(q * QUART, QUART), QUART)

        def part(k):
            zz, yy = k // YS, k % YS
            for cc in range(2):
                hi, lo = split(ham_buf[q, cc, zz, yy])
                rows = pl.ds(pl.multiple_of((k * 2 + cc) * ROWS, ROWS), ROWS)
                ham_hi[rows, cols] = hi
                ham_lo[rows, cols] = lo

        each(0, ZS * YS, part)

    def multiply_left(j):
        wait_bytes(y_in.at[j], yi_recv.at[j])

        def cut(k):
            hi, lo = split(y_in[j, k].reshape(YC * ROWS, HALF))
            rows = pl.ds(pl.multiple_of(k * YC * ROWS, YC * ROWS), YC * ROWS)
            right_cat[rows, 0:HALF] = hi
            right_cat[rows, HALF:WIDE] = lo

        each(0, ZS, cut)

        def tile(k):
            rows = pl.ds(pl.multiple_of(k * TILE, TILE), TILE)
            both = dot(ham_hi[rows, :], right_cat[...])
            value = both[:, HALF:] + dot(ham_lo[rows, :], right_cat[:, 0:HALF]) + both[:, :HALF]
            left[j, pl.ds(k * 2, 2)] = value.reshape(2, YC, ROWS, HALF)

        each(0, N // TILE, tile)

        def send_y(k):
            there, row = other_yc(k)
            remote(
                left.at[j, :, there], y_back.at[j, :, y, :, pl.ds(pl.multiple_of(c * HALF, HALF), HALF)],
                yb_send.at[j], yb_recv.at[j], h, row,
            ).start()

        pltpu.make_async_copy(
            left.at[j, :, yc], y_back.at[j, :, y, :, pl.ds(pl.multiple_of(c * HALF, HALF), HALF)], yb_recv.at[j]
        ).start()
        each(1, YC, send_y)

    def forward_back(j):
        wait_bytes(y_back.at[j], yb_recv.at[j])

        def send_z(k):
            there, row = other_z(k)
            remote(
                y_back.at[j, there], z_back.at[j, pl.ds(z * YS, YS)], zb_send.at[j], zb_recv.at[j], h, row
            ).start()

        pltpu.make_async_copy(y_back.at[j, z], z_back.at[j, pl.ds(z * YS, YS)], zb_recv.at[j]).start()
        each(1, ZS, send_z)

    def multiply_right(k):
        rows = pl.ds(k * (TILE // ROWS), TILE // ROWS)
        hi, lo = split(panels[rows].reshape(TILE, N))

        def columns(q):
            cols = pl.ds(pl.multiple_of(q * TILE, TILE), TILE)
            top = ham_hi[:, cols]
            value = dot(hi, ham_lo[:, cols]) + dot(lo, top) + dot(hi, top)
            value = value.reshape(TILE // ROWS // 2, 2, ROWS, TILE)
            pairs = pl.ds(k * (TILE // ROWS // 2), TILE // ROWS // 2)
            acc[pairs, 0, :, cols] = acc[pairs, 0, :, cols] - value[:, 1]
            acc[pairs, 1, :, cols] = acc[pairs, 1, :, cols] + value[:, 0]

        each(0, N // TILE, columns)

    def decay(a):
        rate = damping[a]
        acc[a, 0] = -(rate * panels[2 * a])
        acc[a, 1] = -(rate * panels[2 * a + 1])

    each(0, OWN, decay)

    lane = lax.broadcasted_iota(jnp.int32, (ROWS, N), 1)
    diagonal = lane == lax.broadcasted_iota(jnp.int32, (ROWS, N), 0) + r * ROWS
    for k in range(BATH):
        columns = jnp.broadcast_to(modes[k : k + 1, :], (ROWS, N))
        row_part = jnp.sum(jnp.where(diagonal, columns, 0.0), axis=1, keepdims=True)
        gap[k] = row_part - columns
        total[k] = row_part + columns

    forward_in(0)
    forward_in(1)
    take_ham(0)
    for d in (1, 3, 2):
        wait_bytes(ham_buf.at[(h + GROUPS - d) % GROUPS, c], h3_recv.at[d - 1])
        to_core(d).start()
    forward_in(2)
    for d in (1, 3, 2):
        take_ham(d)
    multiply_left(0)
    multiply_left(1)
    forward_back(0)
    forward_in(3)
    forward_back(1)
    multiply_left(2)
    forward_back(2)
    multiply_left(3)
    forward_back(3)
    each(0, MATS * ROWS // TILE, multiply_right)

    for d in range(1, GROUPS):
        wait_bytes(pool.at[pl.ds(MATS + (d - 1) * 2 * CAP, 2 * CAP)], pick_recv.at[d - 1])
    names = []
    for d in range(1, GROUPS):
        names += sorted_links(links_vec, h, (h + GROUPS - d) % GROUPS)

    def couple(a):
        real, imag = acc[a, 0], acc[a, 1]
        for slot in range(SLOTS):
            link = links[h * OWN + a, slot]
            mode = bath[h * OWN + a, slot]
            kind = kinds[h * OWN + a, slot]
            place = link - h * OWN
            for i, name in enumerate(names):
                place = jnp.where(link == name, OWN + i, place)
            direct = jnp.where(kind == 1, 1.0, jnp.where(kind == 2, coeff[0, mode], 0.0))
            mixing = jnp.where(kind == 2, coeff[1, mode], 0.0)
            first, second = pool[2 * place], pool[2 * place + 1]
            across = direct * gap[mode]
            along = mixing * total[mode]
            real = real + (across * second + along * first)
            imag = imag + (along * second - across * first)
        acc[a, 0], acc[a, 1] = real, imag

    each(0, OWN, couple)

    stores = []
    for j in range(CHUNKS):
        cols = pl.ds(j * WIDE, WIDE)
        wait_bytes(z_back.at[j], zb_recv.at[j])

        def finish(a, j=j, cols=cols):
            acc[a, 0, :, cols] = acc[a, 0, :, cols] + z_back[j, 2 * a + 1]
            acc[a, 1, :, cols] = acc[a, 1, :, cols] - z_back[j, 2 * a]

        each(0, OWN, finish)
        store = pltpu.make_async_copy(acc.at[:, :, :, cols], deriv.at[:, :, :, cols], out_sem.at[j])
        store.start()
        stores.append(store)

    wait_bytes(ham_buf.at[0, 0, pl.ds(0, ZS - 1), 0], h1_send)
    wait_bytes(ham_buf.at[0, 0, :, pl.ds(0, YS - 1)], h2_send)
    for d in range(GROUPS):
        wait_bytes(ham_buf.at[0, 0], h4_send.at[d])
    for d in range(1, GROUPS):
        wait_bytes(ham_buf.at[0, 0], h3_send.at[d - 1])
        wait_bytes(picked.at[0], pick_send.at[d - 1])
    for j in range(CHUNKS):
        wait_bytes(z_in.at[0, pl.ds(0, ZS - 1)], zi_send.at[j])
        wait_bytes(y_in.at[0, :, pl.ds(0, YC - 1)], yi_send.at[j])
        wait_bytes(left.at[0, :, pl.ds(0, YC - 1)], yb_send.at[j])
        wait_bytes(y_back.at[0, pl.ds(0, ZS - 1)], zb_send.at[j])
    for store in stores:
        store.wait()


def section(rho, incr, ham, modes, coeff, damping, links, bath, kinds):
    vmem = pl.BlockSpec(memory_space=pltpu.VMEM)
    smem = pl.BlockSpec(memory_space=pltpu.SMEM)
    any_space = pl.BlockSpec(memory_space=pl.ANY)
    f32, bf16 = jnp.float32, jnp.bfloat16
    dma = pltpu.SemaphoreType.DMA
    four = (CHUNKS,)
    return pl.pallas_call(
        kernel,
        out_shape=jax.ShapeDtypeStruct((OWN, 2, ROWS, N), f32),
        in_specs=[any_space, any_space, vmem, vmem, vmem, smem, smem, smem, smem, smem],
        out_specs=any_space,
        scratch_shapes=[
            pltpu.VMEM((MATS, ROWS, N), f32),
            pltpu.VMEM((MATS, ROWS, N), f32),
            pltpu.VMEM((MATS, ROWS, N), f32),
            pltpu.VMEM((GROUPS, 2, ZS, YS, ROWS, QUART), f32),
            pltpu.VMEM((N, N), bf16),
            pltpu.VMEM((N, N), bf16),
            pltpu.VMEM((CHUNKS, ZS, YS, ROWS, WIDE), f32),
            pltpu.VMEM((CHUNKS, ZS, YC, ROWS, HALF), f32),
            pltpu.VMEM((N, WIDE), bf16),
            pltpu.VMEM((CHUNKS, ZS, YC, ROWS, HALF), f32),
            pltpu.VMEM((CHUNKS, ZS, YS, ROWS, WIDE), f32),
            pltpu.VMEM((CHUNKS, MATS, ROWS, WIDE), f32),
            pltpu.VMEM((OWN, 2, ROWS, N), f32),
            pltpu.VMEM((MATS + (GROUPS - 1) * 2 * CAP, ROWS, N), f32),
            pltpu.VMEM((GROUPS - 1, 2 * CAP, ROWS, N), f32),
            pltpu.VMEM((BATH, ROWS, N), f32),
            pltpu.VMEM((BATH, ROWS, N), f32),
            dma((2,)),
            dma, dma, dma, dma,
            dma((3,)), dma((3,)), dma(four), dma(four),
            dma(four), dma(four), dma(four), dma(four),
            dma(four), dma(four), dma(four), dma(four),
            dma((3,)), dma((3,)),
            dma(four),
        ],
        compiler_params=pltpu.CompilerParams(
            collective_id=0, has_side_effects=True, vmem_limit_bytes=48 * 1024 * 1024
        ),
        cost_estimate=pl.CostEstimate(flops=6 * 2**30, bytes_accessed=6 * 2**20, transcendentals=0),
        name="section",
    )(rho, incr, ham, modes, links, coeff, damping, links, bath, kinds)


def local(rho, incr, accum, ham, modes, coeff, damping, links, bath, kinds):
    shape = rho.shape
    deriv = section(
        rho.reshape(MATS, ROWS, N), incr.reshape(MATS, ROWS, N), ham, modes, coeff, damping, links, bath, kinds
    ).reshape(shape)
    return (deriv, accum + third_step * deriv)


def solution(mesh):
    in_specs = (
        P("hier", None, "row", None),
        P("hier", None, "row", None),
        P("hier", None, "row", None),
        P("row", None),
        P(),
        P(),
        P("hier"),
        P(),
        P(),
        P(),
    )
    out_specs = (P("hier", None, "row", None), P("hier", None, "row", None))
    return jax.shard_map(local, mesh=mesh, in_specs=in_specs, out_specs=out_specs, check_vma=False)
```

time: 317 us -> 126 us (0.40)
  Pallas kernels: 0 us -> 115 us
  waiting for transfers between devices: 107 us -> 0 us
  local copies, waits for them, and re-layouts: 98.1 us -> 8.15 us
  matrix products: 51.8 us -> 0 us
  other arithmetic: 23.1 us -> 1.75 us
  starting transfers between devices: 20.8 us -> 0 us
  between operations: 14.3 us -> 0.65 us
    pallas_call x0 -> x1, Pallas kernels: none -> 115 us  [section(): pl.pallas_call(kernel, out_shape=jax.ShapeDtypeStruct((OWN, 2, ROWS, N),...]
    all_to_all x2 -> x0, waiting for transfers between devices: 106 us -> none  [the longest x1 59.3 us: local(): lax.all_to_all(tile_rows, 'row', split_axis=2, concat_axis=2, tiled=True)]
    dot_general x14 -> x0, matrix products: 51.8 us -> none  [the longest x1 40 us: local(): jnp.einsum('apdcr,drs->apcs', blocks, ham_blocks, precision=lax.Precision...]
    reshape x5 -> x0, local copies, waits for them, and re-layouts: 41.4 us -> none  [the longest x1 15.2 us: local(): returned.transpose(0, 1, 3, 2, 4).reshape(items, 2, panel_rows, order_size)]
    transpose x2 -> x0, local copies, waits for them, and re-layouts: 22 us -> none  [the longest x1 11.4 us: local(): tile_rows.transpose(0, 1, 3, 4, 2)]
    gather x4 -> x0, local copies, waits for them, and re-layouts: 21.5 us -> none  [local(): neighbour = jnp.take(panel_pool, own_links[:, slot], axis=0)]
    all_to_all x2 -> x0, starting transfers between devices: 20.8 us -> none  [the longest x1 13.6 us: local(): lax.all_to_all(tile_rows, 'row', split_axis=2, concat_axis=2, tiled=True)]
    select_n x4 -> x0, other arithmetic: 11.9 us -> none  [local(): neighbour = jnp.take(panel_pool, own_links[:, slot], axis=0)]
  transfers between devices with their start and end apart: 4 -> 0, of which waited for: 2 -> 0; matrix products, arithmetic and copies ran while one was open for 41% -> 0% of each run, Pallas kernels for 0% -> 0%
where the time goes in v1:
time: 126 us; the launch traced here: 125 us
  Pallas kernels  115 us (91%)
  local copies, waits for them, and re-layouts  8.15 us (6%)
  other arithmetic  1.75 us (1%)
    pallas_call x1, Pallas kernels, section(): pl.pallas_call(kernel, out_shape=jax.ShapeDtypeStruct((OWN, 2, ROWS, N),...  115 us
    unnamed x16, local copies, waits for them, and re-layouts  8.15 us

profile of v1, /device:TPU:1, one launch (start us, length us, event | category | flops | bytes accessed | tf_op | source)
XLA Modules:
  0.0 125.4 jit_solution(11923369780388827545)
XLA Ops:
  0.6 0.8 copy.12.links_vec.links
  1.4 0.8 copy.14.bath
  2.2 0.8 copy.15.kinds
  2.9 0.0 copy-start
  2.9 1.6 %copy-done = f32[16,2,16,1024]{3,2,1,0:T(8,128)S(1)} copy-done((f32[16,2,16,1024]{3,2,1,0:T(8,128)S(1)}, f32[16,2,16,1024]{3,2,1,0:T(8,128)}, u32[]{:S(2)}) %copy-start) | copy-done | bytes 2097176
  4.5 0.0 copy-start.1
  4.5 0.8 copy-done.1
  5.4 0.0 copy-start.2
  5.4 0.8 copy-done.2
  6.1 0.0 copy-start.3
  6.1 0.7 copy-done.3
  6.8 0.0 copy-start.4
  6.8 0.7 copy-done.4
  7.5 0.0 copy-start.5
  7.5 114.9 %section.1 = f32[16,2,16,1024]{3,2,1,0:T(8,128)S(1)} custom-call(f32[32,16,1024]{2,1,0:T(8,128)S(1)} %bitcast.2, f32[32,16,1024]{2,1,0:T(8,128)} %bitcast.3, f32[16,1024]{1,0:T(8,128)S(1)} %copy-done.1, f32[8,1024]{1,0:T(8,128)S(1)} %copy-done.2, s32[64,4]{1,0:T(8,128)S(1)} %copy.12.links_vec.links, f32[2,8]{1,0:T(2,128)S(1)} %copy-done.3, f32[16]{0:T(128)S(1)} %copy-done.4, ...), custom_call_target="tpu_custom_call" | custom-call | flops 6442450944 | bytes 6291456 | tf_op jit(solution)/shard_map/section/pallas_call | solution.py:344
  122.3 0.0 copy-done.5
  122.3 1.8 %multiply_add_fusion = f32[16,2,16,1024]{3,2,1,0:T(8,128)} fusion(f32[16,2,16,1024]{3,2,1,0:T(8,128)S(1)} %copy-done.5, f32[16,2,16,1024]{3,2,1,0:T(8,128)S(1)} %section.1), kind=kLoop, calls=%fused_computation | loop fusion | flops 1048576 | bytes 6291456 | tf_op jit(solution)/shard_map/add | solution.py:388
  124.1 1.3 %copy.17 = f32[16,2,16,1024]{3,2,1,0:T(8,128)} copy(f32[16,2,16,1024]{3,2,1,0:T(8,128)S(1)} %section.1) | data formatting | bytes 4194304
Async XLA Ops:
  2.9 1.6 %copy-start = (f32[16,2,16,1024]{3,2,1,0:T(8,128)S(1)}, f32[16,2,16,1024]{3,2,1,0:T(8,128)}, u32[]{:S(2)}) copy-start(f32[16,2,16,1024]{3,2,1,0:T(8,128)} %param.10) | copy-start | bytes 6291460
  4.5 0.8 copy-start.1
  5.4 0.8 copy-start.2
  6.1 0.7 copy-start.3
  6.8 0.7 copy-start.4
  7.5 114.9 %copy-start.5 = (f32[16,2,16,1024]{3,2,1,0:T(8,128)S(1)}, f32[16,2,16,1024]{3,2,1,0:T(8,128)}, u32[]{:S(2)}) copy-start(f32[16,2,16,1024]{3,2,1,0:T(8,128)} %param.12) | copy-start | bytes 6291460

commit v2 on v1

--- a/solution.py
+++ b/solution.py
@@ -37,23 +37,26 @@
 
 
 def sorted_links(links_vec, rows_of, target):
-    block = links_vec[pl.ds(pl.multiple_of(rows_of * OWN, OWN), OWN), :]
+    block = links_vec[...]
+    member = lax.broadcasted_iota(jnp.int32, block.shape, 1) - rows_of * OWN
+    mine = (member >= 0) & (member < OWN)
     low = target * OWN
     found, last = [], low - 1
     for _ in range(CAP):
-        inside = (block > last) & (block < low + OWN)
+        inside = mine & (block > last) & (block < low + OWN)
         last = jnp.minimum(jnp.min(jnp.where(inside, block, low + OWN - 1)), low + OWN - 1)
         found.append(last)
     return found
 
 
 def kernel(
-    rho, incr, ham, modes, links_vec, coeff, damping, links, bath, kinds,
-    deriv,
+    rho, incr, accum, ham_hbm, modes_hbm, coeff_hbm, damping_hbm, links_hbm, bath_hbm, kinds_hbm,
+    acc, new,
+    ham, modes, coeff, damping, links_vec, links, bath, kinds,
     panels, rho_buf, incr_buf, ham_buf, ham_hi, ham_lo, z_in, y_in, right_cat, left, y_back, z_back,
-    acc, pool, picked, gap, total,
-    load_sem, h1_send, h1_recv, h2_send, h2_recv, h3_send, h3_recv, h4_send, h4_recv,
-    zi_send, zi_recv, yi_send, yi_recv, yb_send, yb_recv, zb_send, zb_recv, pick_send, pick_recv, out_sem,
+    pool, picked, gap, total,
+    rho_sem, incr_sem, load_sem, h1_send, h1_recv, h2_send, h2_recv, h3_send, h3_recv, h4_send, h4_recv,
+    zi_send, zi_recv, yi_send, yi_recv, yb_send, yb_recv, zb_send, zb_recv, pick_send, pick_recv,
 ):
     h = lax.axis_index("hier")
     r = lax.axis_index("row")
@@ -86,10 +89,21 @@
 
         lax.fori_loop(first, last, step, 0)
 
-    load_rho = pltpu.make_async_copy(rho, rho_buf, load_sem.at[0])
-    load_incr = pltpu.make_async_copy(incr, incr_buf, load_sem.at[1])
-    load_rho.start()
-    load_incr.start()
+    def load_panel(j):
+        part = (slice(None), slice(None), pl.ds(j * WIDE, WIDE))
+        return (
+            pltpu.make_async_copy(rho.at[part], rho_buf.at[part], rho_sem.at[j]),
+            pltpu.make_async_copy(incr.at[part], incr_buf.at[part], incr_sem.at[j]),
+        )
+
+    pairs = [
+        (ham_hbm, ham), (modes_hbm, modes), (coeff_hbm, coeff), (damping_hbm, damping), (links_hbm, links_vec),
+        (links_hbm, links), (bath_hbm, bath), (kinds_hbm, kinds), (accum, new),
+    ]
+    loads = [pltpu.make_async_copy(src, dst, load_sem.at[i]) for i, (src, dst) in enumerate(pairs)]
+    for load in load_panel(0):
+        load.start()
+    loads[0].start()
     barrier = pltpu.get_barrier_semaphore()
 
     def greet(group, row):
@@ -99,15 +113,25 @@
     each(1, YC, lambda k: greet(h, other_yc(k)[1]))
     each(1, GROUPS, lambda k: greet((h + k) % GROUPS, r))
 
-    load_rho.wait()
-    load_incr.wait()
-
-    def make_panel(m):
-        value = rho_buf[m] + half_step * incr_buf[m]
-        panels[m] = value
-        pool[m] = value
-
-    each(0, MATS, make_panel)
+    for j in range(1, CHUNKS):
+        for load in load_panel(j):
+            load.start()
+    for load in loads[1:]:
+        load.start()
+
+    def make_panels(j):
+        for load in load_panel(j):
+            load.wait()
+        cols = pl.ds(j * WIDE, WIDE)
+
+        def make(m):
+            part = pl.ds(m * 8, 8)
+            panels[part, :, cols] = rho_buf[part, :, cols] + half_step * incr_buf[part, :, cols]
+
+        each(0, MATS // 8, make)
+
+    make_panels(0)
+    loads[0].wait()
     pl.semaphore_wait(barrier, ZS - 1 + YC - 1 + GROUPS - 1)
 
     ham_own = ham.at[:, pl.ds(pl.multiple_of(h * QUART, QUART), QUART)]
@@ -115,10 +139,12 @@
     h1_local.start()
     each(1, ZS, lambda k: remote(ham_own, ham_buf.at[h, c, z, y], h1_send, h1_recv, h, other_z(k)[1]).start())
 
-    for j in range(CHUNKS):
+    def start_chunk(j):
+        if j == 1:
+            make_panels(j)
         cols = pl.ds(j * WIDE, WIDE)
 
-        def send_z(k, j=j, cols=cols):
+        def send_z(k):
             there, row = other_z(k)
             remote(
                 panels.at[pl.ds(there * YS, YS), :, cols], z_in.at[j, z], zi_send.at[j], zi_recv.at[j], h, row
@@ -127,10 +153,29 @@
         pltpu.make_async_copy(panels.at[pl.ds(z * YS, YS), :, cols], z_in.at[j, z], zi_recv.at[j]).start()
         each(1, ZS, send_z)
 
+    def sent_chunk(j):
+        wait_bytes(z_in.at[0, pl.ds(0, ZS - 1)], zi_send.at[j])
+
+    start_chunk(0)
+    start_chunk(1)
+
     wait_bytes(ham_buf.at[h, c, :, y], h1_recv)
-    own_y = ham_buf.at[h, c, :, y]
-    each(1, YS, lambda k: remote(own_y, own_y, h2_send, h2_recv, h, z * YC + (y + k) % YS * 2 + c).start())
-
+    low, high = pl.ds(0, ZS // 2), pl.ds(ZS // 2, ZS // 2)
+
+    def y_row(k):
+        return z * YC + (y + k) % YS * 2 + c
+
+    for k in (1, 3, 2):
+        part = ham_buf.at[h, c, low, y]
+        remote(part, part, h2_send.at[0], h2_recv.at[0], h, y_row(k)).start()
+        part = ham_buf.at[h, c, high, y]
+        remote(part, part, h2_send.at[1], h2_recv.at[1], (h + k) % GROUPS, r).start()
+
+    for load in loads[1:]:
+        load.wait()
+
+    make_panels(2)
+    make_panels(3)
     for d in range(1, GROUPS):
         chosen = sorted_links(links_vec, (h + d) % GROUPS, h)
         for i in range(CAP):
@@ -138,22 +183,25 @@
             picked[d - 1, 2 * i] = panels[place]
             picked[d - 1, 2 * i + 1] = panels[place + 1]
 
-    wait_bytes(ham_buf.at[h, c, :, pl.ds(0, YS - 1)], h2_recv)
-    for d in (1, 3, 2):
-        remote(
-            ham_buf.at[h, c], ham_buf.at[h, c], h3_send.at[d - 1], h3_recv.at[d - 1], (h + d) % GROUPS, r
-        ).start()
-
-    def to_core(d):
-        quarter = ham_buf.at[(h + GROUPS - d) % GROUPS, c]
-        return remote(quarter, quarter, h4_send.at[d], h4_recv.at[d], h, r - c + 1 - c)
-
-    to_core(0).start()
-    for d in (1, 3, 2):
-        remote(
-            picked.at[d - 1], pool.at[pl.ds(MATS + (d - 1) * 2 * CAP, 2 * CAP)],
-            pick_send.at[d - 1], pick_recv.at[d - 1], (h + d) % GROUPS, r,
-        ).start()
+    def low_part(k, core):
+        return ham_buf.at[(h + GROUPS - k) % GROUPS, core, low]
+
+    def high_part(k, core):
+        return ham_buf.at[:, core, high, (y + YS - k) % YS]
+
+    def to_core(part, i):
+        remote(part, part, h4_send.at[i], h4_recv.at[i], h, r - c + 1 - c).start()
+
+    wait_bytes(ham_buf.at[h, c, low, pl.ds(0, YS - 1)], h2_recv.at[0])
+    for k in (1, 3, 2):
+        part = low_part(0, c)
+        remote(part, part, h3_send.at[k - 1], h3_recv.at[k - 1], (h + k) % GROUPS, r).start()
+    wait_bytes(ham_buf.at[pl.ds(0, GROUPS - 1), c, high, y], h2_recv.at[1])
+    for k in (1, 3, 2):
+        part = high_part(0, c)
+        remote(part, part, h3_send.at[k + 2], h3_recv.at[k + 2], h, y_row(k)).start()
+    to_core(low_part(0, c), 0)
+    to_core(high_part(0, c), GROUPS)
 
     def forward_in(j):
         wait_bytes(z_in.at[j], zi_recv.at[j])
@@ -170,20 +218,23 @@
         ).start()
         each(1, YC, send_y)
 
-    def take_ham(d):
-        q = (h + GROUPS - d) % GROUPS
-        wait_bytes(ham_buf.at[q, 1 - c], h4_recv.at[d])
+    def take(q, k):
         cols = pl.ds(pl.multiple_of(q * QUART, QUART), QUART)
-
-        def part(k):
-            zz, yy = k // YS, k % YS
-            for cc in range(2):
-                hi, lo = split(ham_buf[q, cc, zz, yy])
-                rows = pl.ds(pl.multiple_of((k * 2 + cc) * ROWS, ROWS), ROWS)
-                ham_hi[rows, cols] = hi
-                ham_lo[rows, cols] = lo
-
-        each(0, ZS * YS, part)
+        for cc in range(2):
+            hi, lo = split(ham_buf[q, cc, k // YS, k % YS])
+            rows = pl.ds(pl.multiple_of((k * 2 + cc) * ROWS, ROWS), ROWS)
+            ham_hi[rows, cols] = hi
+            ham_lo[rows, cols] = lo
+
+    def take_low(k):
+        wait_bytes(low_part(k, 1 - c), h4_recv.at[k])
+        q = (h + GROUPS - k) % GROUPS
+        each(0, ZS * YS // 2, lambda i: take(q, i))
+
+    def take_high(k):
+        wait_bytes(high_part(k, 1 - c), h4_recv.at[GROUPS + k])
+        yy = (y + YS - k) % YS
+        each(0, ZS // 2 * GROUPS, lambda i: take(i // (ZS // 2), (ZS // 2 + i % (ZS // 2)) * YS + yy))
 
     def multiply_left(j):
         wait_bytes(y_in.at[j], yi_recv.at[j])
@@ -245,8 +296,11 @@
 
     def decay(a):
         rate = damping[a]
-        acc[a, 0] = -(rate * panels[2 * a])
-        acc[a, 1] = -(rate * panels[2 * a + 1])
+        first, second = panels[2 * a], panels[2 * a + 1]
+        acc[a, 0] = -(rate * first)
+        acc[a, 1] = -(rate * second)
+        pool[2 * a] = first
+        pool[2 * a + 1] = second
 
     each(0, OWN, decay)
 
@@ -258,17 +312,30 @@
         gap[k] = row_part - columns
         total[k] = row_part + columns
 
+    sent_chunk(0)
+    start_chunk(2)
     forward_in(0)
+    sent_chunk(1)
+    start_chunk(3)
     forward_in(1)
-    take_ham(0)
-    for d in (1, 3, 2):
-        wait_bytes(ham_buf.at[(h + GROUPS - d) % GROUPS, c], h3_recv.at[d - 1])
-        to_core(d).start()
-    forward_in(2)
-    for d in (1, 3, 2):
-        take_ham(d)
+    take_low(0)
+    take_high(0)
+    for k in (1, 3, 2):
+        wait_bytes(low_part(k, c), h3_recv.at[k - 1])
+        to_core(low_part(k, c), k)
+        wait_bytes(high_part(k, c), h3_recv.at[k + 2])
+        to_core(high_part(k, c), GROUPS + k)
+    for k in (1, 2, 3):
+        remote(
+            picked.at[k - 1], pool.at[pl.ds(MATS + (k - 1) * 2 * CAP, 2 * CAP)],
+            pick_send.at[k - 1], pick_recv.at[k - 1], (h + k) % GROUPS, r,
+        ).start()
+    for k in (1, 3, 2):
+        take_low(k)
+        take_high(k)
     multiply_left(0)
     multiply_left(1)
+    forward_in(2)
     forward_back(0)
     forward_in(3)
     forward_back(1)
@@ -287,9 +354,9 @@
     def couple(a):
         real, imag = acc[a, 0], acc[a, 1]
         for slot in range(SLOTS):
-            link = links[h * OWN + a, slot]
-            mode = bath[h * OWN + a, slot]
-            kind = kinds[h * OWN + a, slot]
+            link = links[slot, h * OWN + a]
+            mode = bath[slot, h * OWN + a]
+            kind = kinds[slot, h * OWN + a]
             place = link - h * OWN
             for i, name in enumerate(names):
                 place = jnp.where(link == name, OWN + i, place)
@@ -304,49 +371,58 @@
 
     each(0, OWN, couple)
 
-    stores = []
     for j in range(CHUNKS):
         cols = pl.ds(j * WIDE, WIDE)
         wait_bytes(z_back.at[j], zb_recv.at[j])
 
-        def finish(a, j=j, cols=cols):
-            acc[a, 0, :, cols] = acc[a, 0, :, cols] + z_back[j, 2 * a + 1]
-            acc[a, 1, :, cols] = acc[a, 1, :, cols] - z_back[j, 2 * a]
-
-        each(0, OWN, finish)
-        store = pltpu.make_async_copy(acc.at[:, :, :, cols], deriv.at[:, :, :, cols], out_sem.at[j])
-        store.start()
-        stores.append(store)
+        def finish(k, j=j, cols=cols):
+            part = pl.ds(k * 2, 2)
+            back = z_back[j, pl.ds(k * 4, 4)].reshape(2, 2, ROWS, WIDE)
+            real = acc[part, 0, :, cols] + back[:, 1]
+            imag = acc[part, 1, :, cols] - back[:, 0]
+            acc[part, 0, :, cols] = real
+            acc[part, 1, :, cols] = imag
+            new[part, 0, :, cols] = new[part, 0, :, cols] + third_step * real
+            new[part, 1, :, cols] = new[part, 1, :, cols] + third_step * imag
+
+        each(0, OWN // 2, finish)
 
     wait_bytes(ham_buf.at[0, 0, pl.ds(0, ZS - 1), 0], h1_send)
-    wait_bytes(ham_buf.at[0, 0, :, pl.ds(0, YS - 1)], h2_send)
-    for d in range(GROUPS):
-        wait_bytes(ham_buf.at[0, 0], h4_send.at[d])
-    for d in range(1, GROUPS):
-        wait_bytes(ham_buf.at[0, 0], h3_send.at[d - 1])
-        wait_bytes(picked.at[0], pick_send.at[d - 1])
+    wait_bytes(ham_buf.at[0, 0, low, pl.ds(0, YS - 1)], h2_send.at[0])
+    wait_bytes(ham_buf.at[0, 0, high, pl.ds(0, YS - 1)], h2_send.at[1])
+    for k in range(2 * GROUPS - 2):
+        wait_bytes(ham_buf.at[0, 0, low], h3_send.at[k])
+    for k in range(2 * GROUPS):
+        wait_bytes(ham_buf.at[0, 0, low], h4_send.at[k])
+    for k in range(GROUPS - 1):
+        wait_bytes(picked.at[0], pick_send.at[k])
     for j in range(CHUNKS):
-        wait_bytes(z_in.at[0, pl.ds(0, ZS - 1)], zi_send.at[j])
+        if j >= 2:
+            sent_chunk(j)
         wait_bytes(y_in.at[0, :, pl.ds(0, YC - 1)], yi_send.at[j])
         wait_bytes(left.at[0, :, pl.ds(0, YC - 1)], yb_send.at[j])
         wait_bytes(y_back.at[0, pl.ds(0, ZS - 1)], zb_send.at[j])
-    for store in stores:
-        store.wait()
-
-
-def section(rho, incr, ham, modes, coeff, damping, links, bath, kinds):
-    vmem = pl.BlockSpec(memory_space=pltpu.VMEM)
-    smem = pl.BlockSpec(memory_space=pltpu.SMEM)
-    any_space = pl.BlockSpec(memory_space=pl.ANY)
-    f32, bf16 = jnp.float32, jnp.bfloat16
+
+
+def section(*arrays):
+    f32, bf16, i32 = jnp.float32, jnp.bfloat16, jnp.int32
     dma = pltpu.SemaphoreType.DMA
     four = (CHUNKS,)
+    outs = [pltpu.VMEM((OWN, 2, ROWS, N), f32)] * 2
     return pl.pallas_call(
         kernel,
-        out_shape=jax.ShapeDtypeStruct((OWN, 2, ROWS, N), f32),
-        in_specs=[any_space, any_space, vmem, vmem, vmem, smem, smem, smem, smem, smem],
-        out_specs=any_space,
+        out_shape=outs,
+        in_specs=[pl.BlockSpec(memory_space=pltpu.HBM)] * len(arrays),
+        out_specs=[pl.BlockSpec(memory_space=pltpu.VMEM)] * 2,
         scratch_shapes=[
+            pltpu.VMEM((ROWS, N), f32),
+            pltpu.VMEM((BATH, N), f32),
+            pltpu.SMEM((2, BATH), f32),
+            pltpu.SMEM((OWN,), f32),
+            pltpu.VMEM((SLOTS, GROUPS * OWN), i32),
+            pltpu.SMEM((SLOTS, GROUPS * OWN), i32),
+            pltpu.SMEM((SLOTS, GROUPS * OWN), i32),
+            pltpu.SMEM((SLOTS, GROUPS * OWN), i32),
             pltpu.VMEM((MATS, ROWS, N), f32),
             pltpu.VMEM((MATS, ROWS, N), f32),
             pltpu.VMEM((MATS, ROWS, N), f32),
@@ -359,33 +435,56 @@
             pltpu.VMEM((CHUNKS, ZS, YC, ROWS, HALF), f32),
             pltpu.VMEM((CHUNKS, ZS, YS, ROWS, WIDE), f32),
             pltpu.VMEM((CHUNKS, MATS, ROWS, WIDE), f32),
-            pltpu.VMEM((OWN, 2, ROWS, N), f32),
             pltpu.VMEM((MATS + (GROUPS - 1) * 2 * CAP, ROWS, N), f32),
             pltpu.VMEM((GROUPS - 1, 2 * CAP, ROWS, N), f32),
             pltpu.VMEM((BATH, ROWS, N), f32),
             pltpu.VMEM((BATH, ROWS, N), f32),
-            dma((2,)),
-            dma, dma, dma, dma,
-            dma((3,)), dma((3,)), dma(four), dma(four),
+            dma(four), dma(four), dma((9,)),
+            dma, dma, dma((2,)), dma((2,)),
+            dma((6,)), dma((6,)), dma((8,)), dma((8,)),
             dma(four), dma(four), dma(four), dma(four),
             dma(four), dma(four), dma(four), dma(four),
             dma((3,)), dma((3,)),
-            dma(four),
         ],
         compiler_params=pltpu.CompilerParams(
             collective_id=0, has_side_effects=True, vmem_limit_bytes=48 * 1024 * 1024
         ),
         cost_estimate=pl.CostEstimate(flops=6 * 2**30, bytes_accessed=6 * 2**20, transcendentals=0),
         name="section",
-    )(rho, incr, ham, modes, links, coeff, damping, links, bath, kinds)
+    )(*[pltpu.with_memory_space_constraint(array, pltpu.HBM) for array in arrays])
+
+
+def store_kernel(deriv, new, deriv_out, new_out, sem):
+    copies = [
+        pltpu.make_async_copy(deriv, deriv_out, sem.at[0]),
+        pltpu.make_async_copy(new, new_out, sem.at[1]),
+    ]
+    for copy in copies:
+        copy.start()
+    for copy in copies:
+        copy.wait()
+
+
+def store(deriv, new):
+    shape = jax.ShapeDtypeStruct(deriv.shape, deriv.dtype)
+    return pl.pallas_call(
+        store_kernel,
+        out_shape=[shape] * 2,
+        in_specs=[pl.BlockSpec(memory_space=pltpu.VMEM)] * 2,
+        out_specs=[pl.BlockSpec(memory_space=pltpu.HBM)] * 2,
+        scratch_shapes=[pltpu.SemaphoreType.DMA((2,))],
+        compiler_params=pltpu.CompilerParams(vmem_limit_bytes=8 * 1024 * 1024),
+        cost_estimate=pl.CostEstimate(flops=0, bytes_accessed=4 * 2**20, transcendentals=0),
+        name="store",
+    )(*[pltpu.with_memory_space_constraint(array, pltpu.VMEM) for array in (deriv, new)])
 
 
 def local(rho, incr, accum, ham, modes, coeff, damping, links, bath, kinds):
-    shape = rho.shape
-    deriv = section(
-        rho.reshape(MATS, ROWS, N), incr.reshape(MATS, ROWS, N), ham, modes, coeff, damping, links, bath, kinds
-    ).reshape(shape)
-    return (deriv, accum + third_step * deriv)
+    deriv, new = section(
+        rho.reshape(MATS, ROWS, N), incr.reshape(MATS, ROWS, N), accum, ham, modes, coeff, damping,
+        links.T, bath.T, kinds.T,
+    )
+    return store(deriv, new)
 
 
 def solution(mesh):

time: 126 us -> 109 us (0.87)
  local copies, waits for them, and re-layouts: 8.15 us -> 0 us
  Pallas kernels: 115 us -> 108 us
  other arithmetic: 1.75 us -> 0 us
    unnamed x16 -> x0, local copies, waits for them, and re-layouts: 8.15 us -> none
    pallas_call x1 -> x2, Pallas kernels: 115 us -> 108 us  [the longest x1 106 us: section(): pl.pallas_call(kernel, out_shape=outs, in_specs=[pl.BlockSpec(memory_spac...]
    add x1 -> x0, other arithmetic: 1.75 us -> none  [local(): return (deriv, accum + third_step * deriv)]
where the time goes in v2:
time: 109 us
  Pallas kernels  108 us (99%)
    pallas_call x1, Pallas kernels, section(): pl.pallas_call(kernel, out_shape=outs, in_specs=[pl.BlockSpec(memory_spac...  106 us

profile of v2, /device:TPU:1, one launch (start us, length us, event | category | flops | bytes accessed | tf_op | source)
XLA Modules:
  0.0 108.6 jit_solution(15612632184376969840)
XLA Ops:
  0.6 105.9 %section.1 = (f32[16,2,16,1024]{3,2,1,0:T(8,128)S(1)}, f32[16,2,16,1024]{3,2,1,0:T(8,128)S(1)}) custom-call(f32[32,16,1024]{2,1,0:T(8,128)} %bitcast.5, f32[32,16,1024]{2,1,0:T(8,128)} %bitcast.6, f32[16,2,16,1024]{3,2,1,0:T(8,128)} %accum.1, f32[16,1024]{1,0:T(8,128)} %ham_hbm.1, f32[8,1024]{1,0:T(8,128)} %modes_hbm.1, f32[2,8]{1,0:T(2,128)} %coeff_hbm.1, ...), custom_call_target="tpu_custom_call" | custom-call | flops 6442450944 | bytes 6291456 | tf_op jit(solution)/shard_map/section/pallas_call | solution.py:412
  106.6 2.0 %store.1 = (f32[16,2,16,1024]{3,2,1,0:T(8,128)}, f32[16,2,16,1024]{3,2,1,0:T(8,128)}) custom-call(f32[16,2,16,1024]{3,2,1,0:T(8,128)S(1)} %get-tuple-element.4.deriv, f32[16,2,16,1024]{3,2,1,0:T(8,128)S(1)} %get-tuple-element.5.new), custom_call_target="tpu_custom_call" | custom-call | bytes 4194304 | tf_op jit(solution)/shard_map/store/pallas_call | solution.py:470

commit v3 on v2

--- a/solution.py
+++ b/solution.py
@@ -25,6 +25,7 @@
 HALF = WIDE // 2
 QUART = N // GROUPS
 TILE = 256
+PIECES = 4
 
 
 def split(x):
@@ -75,7 +76,7 @@
         pltpu.make_async_copy(ref, ref, sem).wait()
 
     def other_z(k):
-        there = (z + k) % ZS
+        there = (z + ZS // 2 + k // 2 * (2 * (k % 2) - 1) + ZS) % ZS
         return there, there * YC + yc
 
     def other_yc(k):
@@ -101,9 +102,9 @@
         (links_hbm, links), (bath_hbm, bath), (kinds_hbm, kinds), (accum, new),
     ]
     loads = [pltpu.make_async_copy(src, dst, load_sem.at[i]) for i, (src, dst) in enumerate(pairs)]
+    loads[0].start()
     for load in load_panel(0):
         load.start()
-    loads[0].start()
     barrier = pltpu.get_barrier_semaphore()
 
     def greet(group, row):
@@ -113,50 +114,48 @@
     each(1, YC, lambda k: greet(h, other_yc(k)[1]))
     each(1, GROUPS, lambda k: greet((h + k) % GROUPS, r))
 
+    def make_panels(j):
+        for load in load_panel(j):
+            load.wait()
+        cols = pl.ds(j * WIDE, WIDE)
+
+        def make(m):
+            part = pl.ds(m * 8, 8)
+            panels[part, :, cols] = rho_buf[part, :, cols] + half_step * incr_buf[part, :, cols]
+
+        each(0, MATS // 8, make)
+
+    loads[0].wait()
+    pl.semaphore_wait(barrier, ZS - 1 + YC - 1 + GROUPS - 1)
+
+    ham_own = ham.at[:, pl.ds(pl.multiple_of(h * QUART, QUART), QUART)]
+    h1_local = pltpu.make_async_copy(ham_own, ham_buf.at[h, c, z, y], h1_recv)
+    h1_local.start()
+    each(1, ZS, lambda k: remote(ham_own, ham_buf.at[h, c, z, y], h1_send, h1_recv, h, other_z(k)[1]).start())
+
+    def start_chunk(j):
+        if j < 2:
+            make_panels(j)
+        cols = pl.ds(j * WIDE, WIDE)
+
+        def send_z(k):
+            there, row = other_z(k)
+            remote(
+                panels.at[pl.ds(there * YS, YS), :, cols], z_in.at[j, z], zi_send.at[j], zi_recv.at[j], h, row
+            ).start()
+
+        pltpu.make_async_copy(panels.at[pl.ds(z * YS, YS), :, cols], z_in.at[j, z], zi_recv.at[j]).start()
+        each(1, ZS, send_z)
+
+    def sent_chunk(j):
+        wait_bytes(z_in.at[0, pl.ds(0, ZS - 1)], zi_send.at[j])
+
+    start_chunk(0)
     for j in range(1, CHUNKS):
         for load in load_panel(j):
             load.start()
     for load in loads[1:]:
         load.start()
-
-    def make_panels(j):
-        for load in load_panel(j):
-            load.wait()
-        cols = pl.ds(j * WIDE, WIDE)
-
-        def make(m):
-            part = pl.ds(m * 8, 8)
-            panels[part, :, cols] = rho_buf[part, :, cols] + half_step * incr_buf[part, :, cols]
-
-        each(0, MATS // 8, make)
-
-    make_panels(0)
-    loads[0].wait()
-    pl.semaphore_wait(barrier, ZS - 1 + YC - 1 + GROUPS - 1)
-
-    ham_own = ham.at[:, pl.ds(pl.multiple_of(h * QUART, QUART), QUART)]
-    h1_local = pltpu.make_async_copy(ham_own, ham_buf.at[h, c, z, y], h1_recv)
-    h1_local.start()
-    each(1, ZS, lambda k: remote(ham_own, ham_buf.at[h, c, z, y], h1_send, h1_recv, h, other_z(k)[1]).start())
-
-    def start_chunk(j):
-        if j == 1:
-            make_panels(j)
-        cols = pl.ds(j * WIDE, WIDE)
-
-        def send_z(k):
-            there, row = other_z(k)
-            remote(
-                panels.at[pl.ds(there * YS, YS), :, cols], z_in.at[j, z], zi_send.at[j], zi_recv.at[j], h, row
-            ).start()
-
-        pltpu.make_async_copy(panels.at[pl.ds(z * YS, YS), :, cols], z_in.at[j, z], zi_recv.at[j]).start()
-        each(1, ZS, send_z)
-
-    def sent_chunk(j):
-        wait_bytes(z_in.at[0, pl.ds(0, ZS - 1)], zi_send.at[j])
-
-    start_chunk(0)
     start_chunk(1)
 
     wait_bytes(ham_buf.at[h, c, :, y], h1_recv)
@@ -455,10 +454,11 @@
 
 
 def store_kernel(deriv, new, deriv_out, new_out, sem):
-    copies = [
-        pltpu.make_async_copy(deriv, deriv_out, sem.at[0]),
-        pltpu.make_async_copy(new, new_out, sem.at[1]),
-    ]
+    copies = []
+    for i in range(PIECES):
+        part = pl.ds(i * (OWN // PIECES), OWN // PIECES)
+        copies.append(pltpu.make_async_copy(deriv.at[part], deriv_out.at[part], sem.at[0, i]))
+        copies.append(pltpu.make_async_copy(new.at[part], new_out.at[part], sem.at[1, i]))
     for copy in copies:
         copy.start()
     for copy in copies:
@@ -472,7 +472,7 @@
         out_shape=[shape] * 2,
         in_specs=[pl.BlockSpec(memory_space=pltpu.VMEM)] * 2,
         out_specs=[pl.BlockSpec(memory_space=pltpu.HBM)] * 2,
-        scratch_shapes=[pltpu.SemaphoreType.DMA((2,))],
+        scratch_shapes=[pltpu.SemaphoreType.DMA((2, PIECES))],
         compiler_params=pltpu.CompilerParams(vmem_limit_bytes=8 * 1024 * 1024),
         cost_estimate=pl.CostEstimate(flops=0, bytes_accessed=4 * 2**20, transcendentals=0),
         name="store",

time: 109 us -> 108 us (level)
    pallas_call x1, Pallas kernels: 106 us -> 105 us  [section(): pl.pallas_call(kernel, out_shape=outs, in_specs=[pl.BlockSpec(memory_spac...]
where the time goes in v3:
time: 108 us; the launch traced here: 107 us
  Pallas kernels  107 us (99%)
    pallas_call x1, Pallas kernels, section(): pl.pallas_call(kernel, out_shape=outs, in_specs=[pl.BlockSpec(memory_spac...  105 us

profile of v3, /device:TPU:1, one launch (start us, length us, event | category | flops | bytes accessed | tf_op | source)
XLA Modules:
  0.0 107.5 jit_solution(1078734921926609352)
XLA Ops:
  0.6 104.8 %section.1 = (f32[16,2,16,1024]{3,2,1,0:T(8,128)S(1)}, f32[16,2,16,1024]{3,2,1,0:T(8,128)S(1)}) custom-call(f32[32,16,1024]{2,1,0:T(8,128)} %bitcast.5, f32[32,16,1024]{2,1,0:T(8,128)} %bitcast.6, f32[16,2,16,1024]{3,2,1,0:T(8,128)} %accum.1, f32[16,1024]{1,0:T(8,128)} %ham_hbm.1, f32[8,1024]{1,0:T(8,128)} %modes_hbm.1, f32[2,8]{1,0:T(2,128)} %coeff_hbm.1, ...), custom_call_target="tpu_custom_call" | custom-call | flops 6442450944 | bytes 6291456 | tf_op jit(solution)/shard_map/section/pallas_call | solution.py:411
  105.4 2.1 %store.1 = (f32[16,2,16,1024]{3,2,1,0:T(8,128)}, f32[16,2,16,1024]{3,2,1,0:T(8,128)}) custom-call(f32[16,2,16,1024]{3,2,1,0:T(8,128)S(1)} %get-tuple-element.4.deriv, f32[16,2,16,1024]{3,2,1,0:T(8,128)S(1)} %get-tuple-element.5.new), custom_call_target="tpu_custom_call" | custom-call | bytes 4194304 | tf_op jit(solution)/shard_map/store/pallas_call | solution.py:470

commit v4 on v3

--- a/solution.py
+++ b/solution.py
@@ -56,7 +56,7 @@
     ham, modes, coeff, damping, links_vec, links, bath, kinds,
     panels, rho_buf, incr_buf, ham_buf, ham_hi, ham_lo, z_in, y_in, right_cat, left, y_back, z_back,
     pool, picked, gap, total,
-    rho_sem, incr_sem, load_sem, h1_send, h1_recv, h2_send, h2_recv, h3_send, h3_recv, h4_send, h4_recv,
+    line_sem, across_sem, rho_sem, incr_sem, load_sem, h1_send, h1_recv, h2_send, h2_recv, h3_send, h3_recv, h4_send, h4_recv,
     zi_send, zi_recv, yi_send, yi_recv, yb_send, yb_recv, zb_send, zb_recv, pick_send, pick_recv,
 ):
     h = lax.axis_index("hier")
@@ -110,9 +110,16 @@
     def greet(group, row):
         pl.semaphore_signal(barrier, inc=1, device_id=(group, row), device_id_type=MESH)
 
+    def across(body):
+        each(1, YC, lambda k: body(h, other_yc(k)[1]))
+        each(1, GROUPS, lambda k: body((h + k) % GROUPS, r))
+
     each(1, ZS, lambda k: greet(h, other_z(k)[1]))
-    each(1, YC, lambda k: greet(h, other_yc(k)[1]))
-    each(1, GROUPS, lambda k: greet((h + k) % GROUPS, r))
+
+    @pl.when(z == 0)
+    def _():
+        across(greet)
+
 
     def make_panels(j):
         for load in load_panel(j):
@@ -126,7 +133,15 @@
         each(0, MATS // 8, make)
 
     loads[0].wait()
-    pl.semaphore_wait(barrier, ZS - 1 + YC - 1 + GROUPS - 1)
+
+    @pl.when(z == 0)
+    def _():
+        pl.semaphore_wait(barrier, ZS - 1 + YC - 1 + GROUPS - 1)
+
+    @pl.when(z != 0)
+    def _():
+        pl.semaphore_wait(barrier, ZS - 1)
+
 
     ham_own = ham.at[:, pl.ds(pl.multiple_of(h * QUART, QUART), QUART)]
     h1_local = pltpu.make_async_copy(ham_own, ham_buf.at[h, c, z, y], h1_recv)
@@ -147,16 +162,34 @@
         pltpu.make_async_copy(panels.at[pl.ds(z * YS, YS), :, cols], z_in.at[j, z], zi_recv.at[j]).start()
         each(1, ZS, send_z)
 
-    def sent_chunk(j):
-        wait_bytes(z_in.at[0, pl.ds(0, ZS - 1)], zi_send.at[j])
-
     start_chunk(0)
+
+    def signal(sem, group, row):
+        pl.semaphore_signal(sem, inc=1, device_id=(group, row), device_id_type=MESH)
+
+    @pl.when(z == 0)
+    def _():
+        across(lambda group, row: signal(line_sem, group, row))
+
     for j in range(1, CHUNKS):
         for load in load_panel(j):
             load.start()
     for load in loads[1:]:
         load.start()
     start_chunk(1)
+    make_panels(2)
+    make_panels(3)
+    start_chunk(2)
+    start_chunk(3)
+
+    @pl.when(z == 0)
+    def _():
+        pl.semaphore_wait(line_sem, YC - 1 + GROUPS - 1)
+        each(1, ZS, lambda k: signal(across_sem, h, other_z(k)[1]))
+
+    @pl.when(z != 0)
+    def _():
+        pl.semaphore_wait(across_sem, 1)
 
     wait_bytes(ham_buf.at[h, c, :, y], h1_recv)
     low, high = pl.ds(0, ZS // 2), pl.ds(ZS // 2, ZS // 2)
@@ -173,8 +206,6 @@
     for load in loads[1:]:
         load.wait()
 
-    make_panels(2)
-    make_panels(3)
     for d in range(1, GROUPS):
         chosen = sorted_links(links_vec, (h + d) % GROUPS, h)
         for i in range(CAP):
@@ -311,12 +342,7 @@
         gap[k] = row_part - columns
         total[k] = row_part + columns
 
-    sent_chunk(0)
-    start_chunk(2)
     forward_in(0)
-    sent_chunk(1)
-    start_chunk(3)
-    forward_in(1)
     take_low(0)
     take_high(0)
     for k in (1, 3, 2):
@@ -332,15 +358,16 @@
     for k in (1, 3, 2):
         take_low(k)
         take_high(k)
+    forward_in(1)
     multiply_left(0)
     multiply_left(1)
+    forward_back(0)
     forward_in(2)
-    forward_back(0)
+    forward_back(1)
     forward_in(3)
-    forward_back(1)
     multiply_left(2)
+    multiply_left(3)
     forward_back(2)
-    multiply_left(3)
     forward_back(3)
     each(0, MATS * ROWS // TILE, multiply_right)
 
@@ -396,8 +423,7 @@
     for k in range(GROUPS - 1):
         wait_bytes(picked.at[0], pick_send.at[k])
     for j in range(CHUNKS):
-        if j >= 2:
-            sent_chunk(j)
+        wait_bytes(z_in.at[0, pl.ds(0, ZS - 1)], zi_send.at[j])
         wait_bytes(y_in.at[0, :, pl.ds(0, YC - 1)], yi_send.at[j])
         wait_bytes(left.at[0, :, pl.ds(0, YC - 1)], yb_send.at[j])
         wait_bytes(y_back.at[0, pl.ds(0, ZS - 1)], zb_send.at[j])
@@ -438,6 +464,7 @@
             pltpu.VMEM((GROUPS - 1, 2 * CAP, ROWS, N), f32),
             pltpu.VMEM((BATH, ROWS, N), f32),
             pltpu.VMEM((BATH, ROWS, N), f32),
+            pltpu.SemaphoreType.REGULAR, pltpu.SemaphoreType.REGULAR,
             dma(four), dma(four), dma((9,)),
             dma, dma, dma((2,)), dma((2,)),
             dma((6,)), dma((6,)), dma((8,)), dma((8,)),

time: 108 us -> 106 us (0.981)
  Pallas kernels: 107 us -> 105 us
    pallas_call x1, Pallas kernels: 105 us -> 103 us  [section(): pl.pallas_call(kernel, out_shape=outs, in_specs=[pl.BlockSpec(memory_spac...]
where the time goes in v4:
time: 106 us
  Pallas kernels  105 us (99%)
    pallas_call x1, Pallas kernels, section(): pl.pallas_call(kernel, out_shape=outs, in_specs=[pl.BlockSpec(memory_spac...  103 us

profile of v4, /device:TPU:1, one launch (start us, length us, event | category | flops | bytes accessed | tf_op | source)
XLA Modules:
  0.0 105.6 jit_solution(16048162978973602775)
XLA Ops:
  0.6 102.9 %section.1 = (f32[16,2,16,1024]{3,2,1,0:T(8,128)S(1)}, f32[16,2,16,1024]{3,2,1,0:T(8,128)S(1)}) custom-call(f32[32,16,1024]{2,1,0:T(8,128)} %bitcast.5, f32[32,16,1024]{2,1,0:T(8,128)} %bitcast.6, f32[16,2,16,1024]{3,2,1,0:T(8,128)} %accum.1, f32[16,1024]{1,0:T(8,128)} %ham_hbm.1, f32[8,1024]{1,0:T(8,128)} %modes_hbm.1, f32[2,8]{1,0:T(2,128)} %coeff_hbm.1, ...), custom_call_target="tpu_custom_call" | custom-call | flops 6442450944 | bytes 6291456 | tf_op jit(solution)/shard_map/section/pallas_call | solution.py:437
  103.6 2.1 %store.1 = (f32[16,2,16,1024]{3,2,1,0:T(8,128)}, f32[16,2,16,1024]{3,2,1,0:T(8,128)}) custom-call(f32[16,2,16,1024]{3,2,1,0:T(8,128)S(1)} %get-tuple-element.4.deriv, f32[16,2,16,1024]{3,2,1,0:T(8,128)S(1)} %get-tuple-element.5.new), custom_call_target="tpu_custom_call" | custom-call | bytes 4194304 | tf_op jit(solution)/shard_map/store/pallas_call | solution.py:497

commit v5 on v4

--- a/solution.py
+++ b/solution.py
@@ -26,6 +26,8 @@
 QUART = N // GROUPS
 TILE = 256
 PIECES = 4
+LOW = 4
+SPLIT = 4
 
 
 def split(x):
@@ -144,13 +146,18 @@
 
 
     ham_own = ham.at[:, pl.ds(pl.multiple_of(h * QUART, QUART), QUART)]
-    h1_local = pltpu.make_async_copy(ham_own, ham_buf.at[h, c, z, y], h1_recv)
-    h1_local.start()
-    each(1, ZS, lambda k: remote(ham_own, ham_buf.at[h, c, z, y], h1_send, h1_recv, h, other_z(k)[1]).start())
-
-    def start_chunk(j):
-        if j < 2:
-            make_panels(j)
+
+    def ham_along(source, part, offset, sem):
+        dst = ham_buf.at[h, c, source, y]
+        remote(part, dst, h1_send, h1_recv.at[sem], h, (z + offset + ZS) % ZS * YC + yc).start()
+
+    pltpu.make_async_copy(ham_own, ham_buf.at[h, c, z, y], h1_recv.at[2]).start()
+    ham_along(z, ham_own, 2, 0)
+    ham_along(z, ham_own, -2, 1)
+    ham_along(z, ham_own, 1, 2)
+    ham_along(z, ham_own, -1, 2)
+
+    def start_chunk(j, first=1, last=ZS):
         cols = pl.ds(j * WIDE, WIDE)
 
         def send_z(k):
@@ -159,10 +166,12 @@
                 panels.at[pl.ds(there * YS, YS), :, cols], z_in.at[j, z], zi_send.at[j], zi_recv.at[j], h, row
             ).start()
 
-        pltpu.make_async_copy(panels.at[pl.ds(z * YS, YS), :, cols], z_in.at[j, z], zi_recv.at[j]).start()
-        each(1, ZS, send_z)
-
-    start_chunk(0)
+        if first == 1:
+            make_panels(j)
+            pltpu.make_async_copy(panels.at[pl.ds(z * YS, YS), :, cols], z_in.at[j, z], zi_recv.at[j]).start()
+        each(first, last, send_z)
+
+    start_chunk(0, 1, SPLIT)
 
     def signal(sem, group, row):
         pl.semaphore_signal(sem, inc=1, device_id=(group, row), device_id_type=MESH)
@@ -176,11 +185,17 @@
             load.start()
     for load in loads[1:]:
         load.start()
-    start_chunk(1)
-    make_panels(2)
-    make_panels(3)
-    start_chunk(2)
-    start_chunk(3)
+
+    before, behind = (z + ZS - 2) % ZS, (z + 2) % ZS
+    wait_bytes(ham_buf.at[h, c, before, y], h1_recv.at[0])
+    wait_bytes(ham_buf.at[h, c, behind, y], h1_recv.at[1])
+    ham_along(before, ham_buf.at[h, c, before, y], 1, 2)
+    ham_along(behind, ham_buf.at[h, c, behind, y], -1, 2)
+    ham_along(before, ham_buf.at[h, c, before, y], 2, 2)
+
+    start_chunk(0, SPLIT, ZS)
+    for j in range(1, CHUNKS):
+        start_chunk(j)
 
     @pl.when(z == 0)
     def _():
@@ -191,8 +206,8 @@
     def _():
         pl.semaphore_wait(across_sem, 1)
 
-    wait_bytes(ham_buf.at[h, c, :, y], h1_recv)
-    low, high = pl.ds(0, ZS // 2), pl.ds(ZS // 2, ZS // 2)
+    wait_bytes(ham_buf.at[h, c, pl.ds(0, ZS - 2), y], h1_recv.at[2])
+    low, high = pl.ds(0, LOW), pl.ds(LOW, ZS - LOW)
 
     def y_row(k):
         return z * YC + (y + k) % YS * 2 + c
@@ -203,6 +218,18 @@
         part = ham_buf.at[h, c, high, y]
         remote(part, part, h2_send.at[1], h2_recv.at[1], (h + k) % GROUPS, r).start()
 
+    def low_on(y_from):
+        part = ham_buf.at[h, c, low, y_from]
+        for k in (1, 3, 2):
+            remote(part, part, h3_send.at[k - 1], h3_recv.at[k - 1], (h + k) % GROUPS, r).start()
+
+    def high_on(group):
+        part = ham_buf.at[group, c, high, y]
+        for k in (1, 3, 2):
+            remote(part, part, h3_send.at[k + 2], h3_recv.at[k + 2], h, y_row(k)).start()
+
+    low_on(y)
+    high_on(h)
     for load in loads[1:]:
         load.wait()
 
@@ -224,12 +251,10 @@
 
     wait_bytes(ham_buf.at[h, c, low, pl.ds(0, YS - 1)], h2_recv.at[0])
     for k in (1, 3, 2):
-        part = low_part(0, c)
-        remote(part, part, h3_send.at[k - 1], h3_recv.at[k - 1], (h + k) % GROUPS, r).start()
+        low_on((y + k) % YS)
     wait_bytes(ham_buf.at[pl.ds(0, GROUPS - 1), c, high, y], h2_recv.at[1])
     for k in (1, 3, 2):
-        part = high_part(0, c)
-        remote(part, part, h3_send.at[k + 2], h3_recv.at[k + 2], h, y_row(k)).start()
+        high_on((h + k) % GROUPS)
     to_core(low_part(0, c), 0)
     to_core(high_part(0, c), GROUPS)
 
@@ -259,12 +284,12 @@
     def take_low(k):
         wait_bytes(low_part(k, 1 - c), h4_recv.at[k])
         q = (h + GROUPS - k) % GROUPS
-        each(0, ZS * YS // 2, lambda i: take(q, i))
+        each(0, LOW * YS, lambda i: take(q, i))
 
     def take_high(k):
         wait_bytes(high_part(k, 1 - c), h4_recv.at[GROUPS + k])
         yy = (y + YS - k) % YS
-        each(0, ZS // 2 * GROUPS, lambda i: take(i // (ZS // 2), (ZS // 2 + i % (ZS // 2)) * YS + yy))
+        each(0, (ZS - LOW) * GROUPS, lambda i: take(i // (ZS - LOW), (LOW + i % (ZS - LOW)) * YS + yy))
 
     def multiply_left(j):
         wait_bytes(y_in.at[j], yi_recv.at[j])
@@ -277,37 +302,41 @@
 
         each(0, ZS, cut)
 
-        def tile(k):
-            rows = pl.ds(pl.multiple_of(k * TILE, TILE), TILE)
-            both = dot(ham_hi[rows, :], right_cat[...])
-            value = both[:, HALF:] + dot(ham_lo[rows, :], right_cat[:, 0:HALF]) + both[:, :HALF]
-            left[j, pl.ds(k * 2, 2)] = value.reshape(2, YC, ROWS, HALF)
-
-        each(0, N // TILE, tile)
-
-        def send_y(k):
-            there, row = other_yc(k)
+        def half(i):
+            def rows_of(ref):
+                starts = [(z + 2 + i * (ZS // 2) + k) % ZS * (YC * ROWS) for k in range(ZS // 2)]
+                return jnp.concatenate([ref[pl.ds(pl.multiple_of(at, YC * ROWS), YC * ROWS), :] for at in starts], axis=0)
+
+            both = dot(rows_of(ham_hi), right_cat[...])
+            value = both[:, HALF:] + dot(rows_of(ham_lo), right_cat[:, 0:HALF]) + both[:, :HALF]
+            part = pl.ds(i * (ZS // 2), ZS // 2)
+            left[j, part] = value.reshape(ZS // 2, YC, ROWS, HALF)
+            dst = y_back.at[j, part, y, :, pl.ds(pl.multiple_of(c * HALF, HALF), HALF)]
+
+            def send_y(k):
+                there, row = other_yc(k)
+                remote(left.at[j, part, there], dst, yb_send.at[j], yb_recv.at[j, i], h, row).start()
+
+            pltpu.make_async_copy(left.at[j, part, yc], dst, yb_recv.at[j, i]).start()
+            each(1, YC, send_y)
+
+        each(0, 2, half)
+
+    def forward_back(j):
+        def send_z(place):
+            there = (z + 2 + place) % ZS
             remote(
-                left.at[j, :, there], y_back.at[j, :, y, :, pl.ds(pl.multiple_of(c * HALF, HALF), HALF)],
-                yb_send.at[j], yb_recv.at[j], h, row,
+                y_back.at[j, place], z_back.at[j, pl.ds(z * YS, YS)], zb_send.at[j], zb_recv.at[j], h,
+                there * YC + yc,
             ).start()
 
-        pltpu.make_async_copy(
-            left.at[j, :, yc], y_back.at[j, :, y, :, pl.ds(pl.multiple_of(c * HALF, HALF), HALF)], yb_recv.at[j]
-        ).start()
-        each(1, YC, send_y)
-
-    def forward_back(j):
-        wait_bytes(y_back.at[j], yb_recv.at[j])
-
-        def send_z(k):
-            there, row = other_z(k)
-            remote(
-                y_back.at[j, there], z_back.at[j, pl.ds(z * YS, YS)], zb_send.at[j], zb_recv.at[j], h, row
-            ).start()
-
-        pltpu.make_async_copy(y_back.at[j, z], z_back.at[j, pl.ds(z * YS, YS)], zb_recv.at[j]).start()
-        each(1, ZS, send_z)
+        wait_bytes(y_back.at[j, pl.ds(0, ZS // 2)], yb_recv.at[j, 0])
+        for place in (2, 1, 3, 0):
+            send_z(place)
+        wait_bytes(y_back.at[j, pl.ds(ZS // 2, ZS // 2)], yb_recv.at[j, 1])
+        pltpu.make_async_copy(y_back.at[j, ZS - 2], z_back.at[j, pl.ds(z * YS, YS)], zb_recv.at[j]).start()
+        for place in (4, 7, 5):
+            send_z(place)
 
     def multiply_right(k):
         rows = pl.ds(k * (TILE // ROWS), TILE // ROWS)
@@ -355,10 +384,10 @@
             picked.at[k - 1], pool.at[pl.ds(MATS + (k - 1) * 2 * CAP, 2 * CAP)],
             pick_send.at[k - 1], pick_recv.at[k - 1], (h + k) % GROUPS, r,
         ).start()
+    forward_in(1)
     for k in (1, 3, 2):
         take_low(k)
         take_high(k)
-    forward_in(1)
     multiply_left(0)
     multiply_left(1)
     forward_back(0)
@@ -416,10 +445,12 @@
     wait_bytes(ham_buf.at[0, 0, pl.ds(0, ZS - 1), 0], h1_send)
     wait_bytes(ham_buf.at[0, 0, low, pl.ds(0, YS - 1)], h2_send.at[0])
     wait_bytes(ham_buf.at[0, 0, high, pl.ds(0, YS - 1)], h2_send.at[1])
-    for k in range(2 * GROUPS - 2):
-        wait_bytes(ham_buf.at[0, 0, low], h3_send.at[k])
-    for k in range(2 * GROUPS):
-        wait_bytes(ham_buf.at[0, 0, low], h4_send.at[k])
+    for k in range(GROUPS - 1):
+        wait_bytes(low_part(0, 0), h3_send.at[k])
+        wait_bytes(high_part(0, 0), h3_send.at[GROUPS - 1 + k])
+    for k in range(GROUPS):
+        wait_bytes(low_part(0, 0), h4_send.at[k])
+        wait_bytes(high_part(0, 0), h4_send.at[GROUPS + k])
     for k in range(GROUPS - 1):
         wait_bytes(picked.at[0], pick_send.at[k])
     for j in range(CHUNKS):
@@ -466,10 +497,10 @@
             pltpu.VMEM((BATH, ROWS, N), f32),
             pltpu.SemaphoreType.REGULAR, pltpu.SemaphoreType.REGULAR,
             dma(four), dma(four), dma((9,)),
-            dma, dma, dma((2,)), dma((2,)),
+            dma, dma((3,)), dma((2,)), dma((2,)),
             dma((6,)), dma((6,)), dma((8,)), dma((8,)),
             dma(four), dma(four), dma(four), dma(four),
-            dma(four), dma(four), dma(four), dma(four),
+            dma(four), dma((CHUNKS, 2)), dma(four), dma(four),
             dma((3,)), dma((3,)),
         ],
         compiler_params=pltpu.CompilerParams(

time: 106 us -> 105 us (level)
  no operation moved by 1% of the time
where the time goes in v5:
time: 105 us
  Pallas kernels  104 us (99%)
    pallas_call x1, Pallas kernels, section(): pl.pallas_call(kernel, out_shape=outs, in_specs=[pl.BlockSpec(memory_spac...  102 us

profile of v5, /device:TPU:1, one launch (start us, length us, event | category | flops | bytes accessed | tf_op | source)
XLA Modules:
  0.0 104.8 jit_solution(1929044458308338963)
XLA Ops:
  0.6 102.1 %section.1 = (f32[16,2,16,1024]{3,2,1,0:T(8,128)S(1)}, f32[16,2,16,1024]{3,2,1,0:T(8,128)S(1)}) custom-call(f32[32,16,1024]{2,1,0:T(8,128)} %bitcast.5, f32[32,16,1024]{2,1,0:T(8,128)} %bitcast.6, f32[16,2,16,1024]{3,2,1,0:T(8,128)} %accum.1, f32[16,1024]{1,0:T(8,128)} %ham_hbm.1, f32[8,1024]{1,0:T(8,128)} %modes_hbm.1, f32[2,8]{1,0:T(2,128)} %coeff_hbm.1, ...), custom_call_target="tpu_custom_call" | custom-call | flops 6442450944 | bytes 6291456 | tf_op jit(solution)/shard_map/section/pallas_call | solution.py:468
  102.8 2.1 %store.1 = (f32[16,2,16,1024]{3,2,1,0:T(8,128)}, f32[16,2,16,1024]{3,2,1,0:T(8,128)}) custom-call(f32[16,2,16,1024]{3,2,1,0:T(8,128)S(1)} %get-tuple-element.4.deriv, f32[16,2,16,1024]{3,2,1,0:T(8,128)S(1)} %get-tuple-element.5.new), custom_call_target="tpu_custom_call" | custom-call | bytes 4194304 | tf_op jit(solution)/shard_map/store/pallas_call | solution.py:528

commit v6 on v5

--- a/solution.py
+++ b/solution.py
@@ -104,19 +104,19 @@
         (links_hbm, links), (bath_hbm, bath), (kinds_hbm, kinds), (accum, new),
     ]
     loads = [pltpu.make_async_copy(src, dst, load_sem.at[i]) for i, (src, dst) in enumerate(pairs)]
+    barrier = pltpu.get_barrier_semaphore()
+
+    def greet(group, row):
+        pl.semaphore_signal(barrier, inc=1, device_id=(group, row), device_id_type=MESH)
+
+    def across(body):
+        each(1, YC, lambda k: body(h, other_yc(k)[1]))
+        each(1, GROUPS, lambda k: body((h + k) % GROUPS, r))
+
+    each(1, ZS, lambda k: greet(h, other_z(k)[1]))
     loads[0].start()
     for load in load_panel(0):
         load.start()
-    barrier = pltpu.get_barrier_semaphore()
-
-    def greet(group, row):
-        pl.semaphore_signal(barrier, inc=1, device_id=(group, row), device_id_type=MESH)
-
-    def across(body):
-        each(1, YC, lambda k: body(h, other_yc(k)[1]))
-        each(1, GROUPS, lambda k: body((h + k) % GROUPS, r))
-
-    each(1, ZS, lambda k: greet(h, other_z(k)[1]))
 
     @pl.when(z == 0)
     def _():
@@ -147,9 +147,11 @@
 
     ham_own = ham.at[:, pl.ds(pl.multiple_of(h * QUART, QUART), QUART)]
 
+    turn = 1 - 2 * c
+
     def ham_along(source, part, offset, sem):
         dst = ham_buf.at[h, c, source, y]
-        remote(part, dst, h1_send, h1_recv.at[sem], h, (z + offset + ZS) % ZS * YC + yc).start()
+        remote(part, dst, h1_send, h1_recv.at[sem], h, (z + offset * turn + ZS) % ZS * YC + yc).start()
 
     pltpu.make_async_copy(ham_own, ham_buf.at[h, c, z, y], h1_recv.at[2]).start()
     ham_along(z, ham_own, 2, 0)
@@ -186,7 +188,7 @@
     for load in loads[1:]:
         load.start()
 
-    before, behind = (z + ZS - 2) % ZS, (z + 2) % ZS
+    before, behind = (z + ZS - 2 * turn) % ZS, (z + ZS + 2 * turn) % ZS
     wait_bytes(ham_buf.at[h, c, before, y], h1_recv.at[0])
     wait_bytes(ham_buf.at[h, c, behind, y], h1_recv.at[1])
     ham_along(before, ham_buf.at[h, c, before, y], 1, 2)
@@ -415,6 +417,7 @@
             place = link - h * OWN
             for i, name in enumerate(names):
                 place = jnp.where(link == name, OWN + i, place)
+            place = jnp.clip(place, 0, OWN + (GROUPS - 1) * CAP - 1)
             direct = jnp.where(kind == 1, 1.0, jnp.where(kind == 2, coeff[0, mode], 0.0))
             mixing = jnp.where(kind == 2, coeff[1, mode], 0.0)
             first, second = pool[2 * place], pool[2 * place + 1]

time: 105 us -> 105 us (level)
  no operation moved by 1% of the time
where the time goes in v6:
time: 105 us
  Pallas kernels  104 us (99%)
    pallas_call x1, Pallas kernels, section(): pl.pallas_call(kernel, out_shape=outs, in_specs=[pl.BlockSpec(memory_spac...  102 us

profile of v6, /device:TPU:1, one launch (start us, length us, event | category | flops | bytes accessed | tf_op | source)
XLA Modules:
  0.0 104.7 jit_solution(31777542191506190)
XLA Ops:
  0.6 102.0 %section.1 = (f32[16,2,16,1024]{3,2,1,0:T(8,128)S(1)}, f32[16,2,16,1024]{3,2,1,0:T(8,128)S(1)}) custom-call(f32[32,16,1024]{2,1,0:T(8,128)} %bitcast.5, f32[32,16,1024]{2,1,0:T(8,128)} %bitcast.6, f32[16,2,16,1024]{3,2,1,0:T(8,128)} %accum.1, f32[16,1024]{1,0:T(8,128)} %ham_hbm.1, f32[8,1024]{1,0:T(8,128)} %modes_hbm.1, f32[2,8]{1,0:T(2,128)} %coeff_hbm.1, ...), custom_call_target="tpu_custom_call" | custom-call | flops 6442450944 | bytes 6291456 | tf_op jit(solution)/shard_map/section/pallas_call | solution.py:471
  102.6 2.1 %store.1 = (f32[16,2,16,1024]{3,2,1,0:T(8,128)}, f32[16,2,16,1024]{3,2,1,0:T(8,128)}) custom-call(f32[16,2,16,1024]{3,2,1,0:T(8,128)S(1)} %get-tuple-element.4.deriv, f32[16,2,16,1024]{3,2,1,0:T(8,128)S(1)} %get-tuple-element.5.new), custom_call_target="tpu_custom_call" | custom-call | bytes 4194304 | tf_op jit(solution)/shard_map/store/pallas_call | solution.py:531

commit v7 on v6

--- a/solution.py
+++ b/solution.py
@@ -25,7 +25,7 @@
 HALF = WIDE // 2
 QUART = N // GROUPS
 TILE = 256
-PIECES = 4
+PIECES = 1
 LOW = 4
 SPLIT = 4
 
@@ -429,8 +429,29 @@
 
     each(0, OWN, couple)
 
+    def wait_sent():
+        wait_bytes(ham_buf.at[0, 0, pl.ds(0, ZS - 1), 0], h1_send)
+        wait_bytes(ham_buf.at[0, 0, low, pl.ds(0, YS - 1)], h2_send.at[0])
+        wait_bytes(ham_buf.at[0, 0, high, pl.ds(0, YS - 1)], h2_send.at[1])
+        for k in range(GROUPS - 1):
+            wait_bytes(low_part(0, 0), h3_send.at[k])
+            wait_bytes(high_part(0, 0), h3_send.at[GROUPS - 1 + k])
+        for k in range(GROUPS):
+            wait_bytes(low_part(0, 0), h4_send.at[k])
+            wait_bytes(high_part(0, 0), h4_send.at[GROUPS + k])
+        for k in range(GROUPS - 1):
+            wait_bytes(picked.at[0], pick_send.at[k])
+        for j in range(CHUNKS):
+            wait_bytes(z_in.at[0, pl.ds(0, ZS - 1)], zi_send.at[j])
+            wait_bytes(y_in.at[0, :, pl.ds(0, YC - 1)], yi_send.at[j])
+            wait_bytes(left.at[0, :, pl.ds(0, YC - 1)], yb_send.at[j])
+            if j < CHUNKS - 1:
+                wait_bytes(y_back.at[0, pl.ds(0, ZS - 1)], zb_send.at[j])
+
     for j in range(CHUNKS):
         cols = pl.ds(j * WIDE, WIDE)
+        if j == CHUNKS - 1:
+            wait_sent()
         wait_bytes(z_back.at[j], zb_recv.at[j])
 
         def finish(k, j=j, cols=cols):
@@ -445,22 +466,7 @@
 
         each(0, OWN // 2, finish)
 
-    wait_bytes(ham_buf.at[0, 0, pl.ds(0, ZS - 1), 0], h1_send)
-    wait_bytes(ham_buf.at[0, 0, low, pl.ds(0, YS - 1)], h2_send.at[0])
-    wait_bytes(ham_buf.at[0, 0, high, pl.ds(0, YS - 1)], h2_send.at[1])
-    for k in range(GROUPS - 1):
-        wait_bytes(low_part(0, 0), h3_send.at[k])
-        wait_bytes(high_part(0, 0), h3_send.at[GROUPS - 1 + k])
-    for k in range(GROUPS):
-        wait_bytes(low_part(0, 0), h4_send.at[k])
-        wait_bytes(high_part(0, 0), h4_send.at[GROUPS + k])
-    for k in range(GROUPS - 1):
-        wait_bytes(picked.at[0], pick_send.at[k])
-    for j in range(CHUNKS):
-        wait_bytes(z_in.at[0, pl.ds(0, ZS - 1)], zi_send.at[j])
-        wait_bytes(y_in.at[0, :, pl.ds(0, YC - 1)], yi_send.at[j])
-        wait_bytes(left.at[0, :, pl.ds(0, YC - 1)], yb_send.at[j])
-        wait_bytes(y_back.at[0, pl.ds(0, ZS - 1)], zb_send.at[j])
+    wait_bytes(y_back.at[0, pl.ds(0, ZS - 1)], zb_send.at[CHUNKS - 1])
 
 
 def section(*arrays):

time: 105 us -> 105 us (level)
  no operation moved by 1% of the time
where the time goes in v7:
time: 105 us
  Pallas kernels  104 us (99%)
    pallas_call x1, Pallas kernels, section(): pl.pallas_call(kernel, out_shape=outs, in_specs=[pl.BlockSpec(memory_spac...  102 us

profile of v7, /device:TPU:1, one launch (start us, length us, event | category | flops | bytes accessed | tf_op | source)
XLA Modules:
  0.0 104.6 jit_solution(17575562286955027477)
XLA Ops:
  0.6 101.9 %section.1 = (f32[16,2,16,1024]{3,2,1,0:T(8,128)S(1)}, f32[16,2,16,1024]{3,2,1,0:T(8,128)S(1)}) custom-call(f32[32,16,1024]{2,1,0:T(8,128)} %bitcast.5, f32[32,16,1024]{2,1,0:T(8,128)} %bitcast.6, f32[16,2,16,1024]{3,2,1,0:T(8,128)} %accum.1, f32[16,1024]{1,0:T(8,128)} %ham_hbm.1, f32[8,1024]{1,0:T(8,128)} %modes_hbm.1, f32[2,8]{1,0:T(2,128)} %coeff_hbm.1, ...), custom_call_target="tpu_custom_call" | custom-call | flops 6442450944 | bytes 6291456 | tf_op jit(solution)/shard_map/section/pallas_call | solution.py:477
  102.6 2.0 %store.1 = (f32[16,2,16,1024]{3,2,1,0:T(8,128)}, f32[16,2,16,1024]{3,2,1,0:T(8,128)}) custom-call(f32[16,2,16,1024]{3,2,1,0:T(8,128)S(1)} %get-tuple-element.4.deriv, f32[16,2,16,1024]{3,2,1,0:T(8,128)S(1)} %get-tuple-element.5.new), custom_call_target="tpu_custom_call" | custom-call | bytes 4194304 | tf_op jit(solution)/shard_map/store/pallas_call | solution.py:537

commit v8 on v6

--- a/solution.py
+++ b/solution.py
@@ -78,7 +78,7 @@
         pltpu.make_async_copy(ref, ref, sem).wait()
 
     def other_z(k):
-        there = (z + ZS // 2 + k // 2 * (2 * (k % 2) - 1) + ZS) % ZS
+        there = (z + ZS // 2 + k // 2 * (2 * (k % 2) - 1) * (1 - 2 * c) + ZS) % ZS
         return there, there * YC + yc
 
     def other_yc(k):

time: 105 us -> 105 us (level)
  no operation moved by 1% of the time
where the time goes in v8:
time: 105 us
  Pallas kernels  104 us (99%)
    pallas_call x1, Pallas kernels, section(): pl.pallas_call(kernel, out_shape=outs, in_specs=[pl.BlockSpec(memory_spac...  102 us

profile of v8, /device:TPU:1, one launch (start us, length us, event | category | flops | bytes accessed | tf_op | source)
XLA Modules:
  0.0 104.7 jit_solution(7225213125744160663)
XLA Ops:
  0.6 102.0 %section.1 = (f32[16,2,16,1024]{3,2,1,0:T(8,128)S(1)}, f32[16,2,16,1024]{3,2,1,0:T(8,128)S(1)}) custom-call(f32[32,16,1024]{2,1,0:T(8,128)} %bitcast.5, f32[32,16,1024]{2,1,0:T(8,128)} %bitcast.6, f32[16,2,16,1024]{3,2,1,0:T(8,128)} %accum.1, f32[16,1024]{1,0:T(8,128)} %ham_hbm.1, f32[8,1024]{1,0:T(8,128)} %modes_hbm.1, f32[2,8]{1,0:T(2,128)} %coeff_hbm.1, ...), custom_call_target="tpu_custom_call" | custom-call | flops 6442450944 | bytes 6291456 | tf_op jit(solution)/shard_map/section/pallas_call | solution.py:471
  102.6 2.1 %store.1 = (f32[16,2,16,1024]{3,2,1,0:T(8,128)}, f32[16,2,16,1024]{3,2,1,0:T(8,128)}) custom-call(f32[16,2,16,1024]{3,2,1,0:T(8,128)S(1)} %get-tuple-element.4.deriv, f32[16,2,16,1024]{3,2,1,0:T(8,128)S(1)} %get-tuple-element.5.new), custom_call_target="tpu_custom_call" | custom-call | bytes 4194304 | tf_op jit(solution)/shard_map/store/pallas_call | solution.py:531
